TPU v7x, 32 devices: a whole 2x2x4 slice. The times are simulated.
32 devices in a mesh: ta: 4 (over z), ha: 2 (over y), wa: 4 (over x, core).
Axes of the slice: x: 2, y: 2, z: 4, core: 2. Of those that a mesh axis runs over, the one named last changes fastest.
Arguments:
- stream: bfloat16 [4, 2, 384, 1536], P('ta', 'ha'), may hold values from -40 to 40
- queries: bfloat16 [4, 2, 384, 1536], P('ta', 'ha', None, 'wa'), may hold values from -6 to 6
- key_heads: bfloat16 [4, 2, 384, 1536], P('ta', 'ha', None, 'wa'), may hold values from -6 to 6
- value_heads: bfloat16 [4, 2, 384, 1536], P('ta', 'ha', None, 'wa'), may hold values from -6 to 6
- out_weight: bfloat16 [1536, 1536], P('wa'), may hold values from -0.15625 to 0.15625
- norm_gain: float32 [1536], replicated, may hold values from 0.25 to 1.75
- up_weight: bfloat16 [1536, 6144], P(('ta', 'ha'), 'wa'), may hold values from -0.15625 to 0.15625
- down_weight: bfloat16 [6144, 1536], P('wa', ('ta', 'ha')), may hold values from -0.078125 to 0.078125
- tile_route: int32 [4, 2, 1], P('ta', 'ha'), may hold values 0 or 1
- cotangent: bfloat16 [4, 2, 384, 1536], P('ta', 'ha'), may hold values from -6 to 6
Outputs:
- stream_grad: bfloat16 [4, 2, 384, 1536], P('ta', 'ha')
- query_grad: bfloat16 [4, 2, 384, 1536], P('ta', 'ha', None, 'wa')
- key_grad: bfloat16 [4, 2, 384, 1536], P('ta', 'ha', None, 'wa')
- value_grad: bfloat16 [4, 2, 384, 1536], P('ta', 'ha', None, 'wa')
- out_weight_grad: float32 [1536, 1536], P('wa', ('ta', 'ha'))
All inputs are finite; a program needn't handle non-finite values. No bound on the sum of `tile_route` on one device may be relied on, other than what follows from the above.
Results may differ from a plain program's by a relative error of at most 0.014.
Values may be sent and summed in bfloat16 or wider, within the bound.
A program may use at most 128 MiB of HBM per device.

v0:
```python
import math

import jax
import jax.numpy as jnp
from jax import lax
from jax.sharding import PartitionSpec as P

HS = 128
TILE = 384


EPSILON = 1e-06
TANH_SCALE = 0.7978845608028654
CUBIC_COEF = 0.044715
NEG_FILL = -1e30


def extended(cells, sides, width):
    for axis, dim in sides:
        count = lax.axis_size(axis)
        ends = count - 1
        head = lax.slice_in_dim(cells, 0, width, axis=dim)
        tail = lax.slice_in_dim(cells, cells.shape[dim] - width, cells.shape[dim], axis=dim)
        cells = jnp.concatenate(
            [
                lax.ppermute(tail, axis, [(i, (i + 1) % count) for i in range(ends)]),
                cells,
                lax.ppermute(head, axis, [((i + 1) % count, i) for i in range(ends)]),
            ],
            axis=dim,
        )
    return cells


def from_behind(array, axis, by):
    devices = lax.axis_size(axis)
    pairs = [(i, i + by) for i in range(devices) if 0 <= i + by < devices]
    return lax.ppermute(array, axis, pairs)


def gelu_slope(pre_act):
    tanh_arg = TANH_SCALE * (pre_act + CUBIC_COEF * pre_act * pre_act * pre_act)
    tanh_val = jnp.tanh(tanh_arg)
    return 0.5 * (1.0 + tanh_val) + 0.5 * pre_act * (1.0 - tanh_val * tanh_val) * TANH_SCALE * (
        1.0 + 3.0 * CUBIC_COEF * pre_act * pre_act
    )


def head_probs(query_rows, key_rows, key_marks, score_scale):
    scores = (
        jnp.einsum("qd,kd->qk", query_rows, key_rows, preferred_element_type=jnp.float32)
        * score_scale
    )
    scores = jnp.where(key_marks[None, :] > 0.5, scores, NEG_FILL)
    row_max = jnp.max(scores, axis=1)
    weights = jnp.exp(scores - row_max[:, None])
    row_total = jnp.sum(weights, axis=1)
    return (weights / row_total[:, None], row_max, row_total)


def layer_norm(residual):
    mean_val = jnp.mean(residual, axis=1, keepdims=True)
    centered = residual - mean_val
    variance = jnp.mean(centered * centered, axis=1, keepdims=True)
    inv_std = lax.rsqrt(variance + EPSILON)
    return (centered * inv_std, inv_std)


def norm_backward(norm_grad, norm_gain, normed, inv_std):
    scaled = norm_grad * norm_gain
    return (
        scaled
        - jnp.mean(scaled, axis=1, keepdims=True)
        - normed * jnp.mean(scaled * normed, axis=1, keepdims=True)
    ) * inv_std


def shards(
    stream,
    queries,
    key_heads,
    value_heads,
    out_weight,
    norm_gain,
    up_weight,
    down_weight,
    tile_route,
    cotangent,
):
    row_count = stream.shape[2]
    model_width = stream.shape[3]
    channels = queries.shape[3]
    heads_here = channels // HS
    tile_count = row_count // TILE
    score_scale = 1.0 / math.sqrt(HS)
    tile_ids = jnp.arange(tile_count, dtype=jnp.int32)
    tile_marks = tile_route.astype(jnp.bfloat16)
    faces_key, faces_value, faces_marks = (
        extended(key_heads, (("ta", 0), ("ha", 1)), 1),
        extended(value_heads, (("ta", 0), ("ha", 1)), 1),
        extended(tile_marks, (("ta", 0), ("ha", 1)), 1),
    )

    def window():
        key_block = faces_key.reshape(9 * TILE, heads_here, HS)
        value_block = faces_value.reshape(9 * TILE, heads_here, HS)
        mark_block = faces_marks.reshape(9).astype(jnp.float32)
        key_marks = jnp.repeat(mark_block, TILE)
        query_tile = queries.reshape(TILE, heads_here, HS)
        return (
            query_tile.transpose(1, 0, 2),
            key_block.transpose(1, 0, 2),
            value_block.transpose(1, 0, 2),
            key_marks,
        )

    def forward_tile(tile_index):
        own_mark = tile_marks[0, 0, tile_index]
        query_tile, key_block, value_block, key_marks = window()

        def per_head(operands):
            query_rows, key_rows, value_rows = operands
            weights, row_max, row_total = head_probs(query_rows, key_rows, key_marks, score_scale)
            mixture = jnp.dot(
                weights.astype(jnp.bfloat16), value_rows, preferred_element_type=jnp.float32
            )
            return (mixture, row_max, row_total)

        mixture, row_max, row_total = lax.map(per_head, (query_tile, key_block, value_block))
        scaled = (mixture * own_mark.astype(jnp.float32)).astype(jnp.bfloat16)
        return (scaled.transpose(1, 0, 2).reshape(TILE, channels), row_max, row_total)

    attn_tiles, max_tiles, total_tiles = lax.map(forward_tile, tile_ids)
    attention = attn_tiles.reshape(row_count, channels)
    attn_part = jnp.dot(attention, out_weight, preferred_element_type=jnp.float32)
    head_share = lax.psum_scatter(attn_part, "wa", scatter_dimension=0, tiled=True)
    share_rows = head_share.shape[0]
    share_start = lax.axis_index("wa") * share_rows
    flat_stream = stream.reshape(row_count, model_width)
    flat_cot = cotangent.reshape(row_count, model_width)
    residual = (
        lax.dynamic_slice_in_dim(flat_stream, share_start, share_rows, 0).astype(jnp.float32)
        + head_share
    )
    normed, inv_std = layer_norm(residual)
    hidden_share = (normed * norm_gain).astype(jnp.bfloat16)
    hidden_in = lax.all_gather(hidden_share, "wa", axis=0, tiled=True)
    up_full, down_full = (
        lax.all_gather(up_weight, ("ta", "ha"), axis=0, tiled=True),
        lax.all_gather(down_weight, ("ta", "ha"), axis=1, tiled=True),
    )
    pre_act = jnp.dot(hidden_in, up_full, preferred_element_type=jnp.float32)
    act_grad = jnp.einsum("td,fd->tf", flat_cot, down_full, preferred_element_type=jnp.float32)
    pre_grad = (act_grad * gelu_slope(pre_act)).astype(jnp.bfloat16)
    norm_part = jnp.einsum("tf,df->td", pre_grad, up_full, preferred_element_type=jnp.float32)
    norm_share = lax.psum_scatter(norm_part, "wa", scatter_dimension=0, tiled=True)
    cot_share = lax.dynamic_slice_in_dim(flat_cot, share_start, share_rows, 0).astype(jnp.float32)
    grad_share = (cot_share + norm_backward(norm_share, norm_gain, normed, inv_std)).astype(
        jnp.bfloat16
    )
    stream_grad = lax.all_gather(grad_share, "wa", axis=0, tiled=True)
    weight_part = jnp.einsum(
        "tc,td->cd", attention, stream_grad, preferred_element_type=jnp.float32
    )
    out_weight_grad = lax.psum_scatter(weight_part, ("ta", "ha"), scatter_dimension=1, tiled=True)
    attn_grad = jnp.einsum(
        "td,cd->tc", stream_grad, out_weight, preferred_element_type=jnp.float32
    ).astype(jnp.bfloat16)
    row_marks = jnp.repeat(tile_marks.reshape(tile_count), TILE)
    masked_grad = attn_grad * row_marks[:, None]

    def own_side():
        query_tile, key_block, value_block, key_marks = window()
        grad_tile = masked_grad.reshape(TILE, heads_here, HS).transpose(1, 0, 2)

        def head_back(operands):
            query_rows, key_rows, value_rows, grad_rows = operands
            weights = head_probs(query_rows, key_rows, key_marks, score_scale)[0]
            grad_probs = jnp.einsum(
                "qd,kd->qk", grad_rows, value_rows, preferred_element_type=jnp.float32
            )
            row_delta = jnp.sum(weights * grad_probs, axis=1)
            grad_scores = (weights * (grad_probs - row_delta[:, None]) * score_scale).astype(
                jnp.bfloat16
            )
            query_part = jnp.dot(grad_scores, key_rows, preferred_element_type=jnp.float32).astype(
                jnp.bfloat16
            )
            value_part = jnp.einsum(
                "qk,qd->kd",
                weights.astype(jnp.bfloat16),
                grad_rows,
                preferred_element_type=jnp.float32,
            ).astype(jnp.bfloat16)
            key_part = jnp.einsum(
                "qk,qd->kd", grad_scores, query_rows, preferred_element_type=jnp.float32
            ).astype(jnp.bfloat16)
            return (query_part, row_delta, key_part, value_part)

        results = lax.map(head_back, (query_tile, key_block, value_block, grad_tile))
        query_part = results[0].transpose(1, 0, 2).reshape(TILE, channels)
        key_part = results[2].transpose(1, 0, 2).reshape(3, 3, TILE, channels)
        value_part = results[3].transpose(1, 0, 2).reshape(3, 3, TILE, channels)
        return (query_part, results[1], key_part, value_part)

    def guarded_own():
        blank_parts = (
            jnp.zeros((TILE, channels), jnp.bfloat16),
            jnp.zeros((heads_here, TILE), jnp.float32),
        )
        blank_parts = blank_parts + (
            jnp.zeros((3, 3, TILE, channels), jnp.bfloat16),
            jnp.zeros((3, 3, TILE, channels), jnp.bfloat16),
        )
        return own_side()

    def place_tile(carried, tile_index):
        query_part, row_delta, key_part, value_part = guarded_own()
        return ((key_part, value_part), query_part)

    empty_slots = jnp.zeros((3, 3, row_count, channels), jnp.bfloat16)
    (slots_key, slots_value), query_parts = lax.scan(
        place_tile, (empty_slots, empty_slots), tile_ids
    )
    middle_key = slots_key[1].astype(jnp.float32)
    middle_value = slots_value[1].astype(jnp.float32)
    for by_step, source in ((-1, 0), (1, 2)):
        moved_key, moved_value = from_behind(
            (slots_key[source], slots_value[source]), "ta", by_step
        )
        middle_key = middle_key + moved_key.astype(jnp.float32)
        middle_value = middle_value + moved_value.astype(jnp.float32)
    final_key = middle_key[1]
    final_value = middle_value[1]
    for by_step, source in ((-1, 0), (1, 2)):
        moved_key, moved_value = (
            from_behind(middle_key[source].astype(jnp.bfloat16), "ha", by_step).astype(jnp.float32),
            from_behind(middle_value[source].astype(jnp.bfloat16), "ha", by_step).astype(
                jnp.float32
            ),
        )
        final_key = final_key + moved_key
        final_value = final_value + moved_value
    key_grad = final_key.astype(jnp.bfloat16).reshape(1, 1, row_count, channels)
    value_grad = final_value.astype(jnp.bfloat16).reshape(1, 1, row_count, channels)
    query_grad = query_parts.reshape(1, 1, row_count, channels)
    return (
        stream_grad.reshape(1, 1, row_count, model_width),
        query_grad,
        key_grad,
        value_grad,
        out_weight_grad,
    )


def solution(mesh):
    placed = (
        P("ta", "ha", None, None),
        P("ta", "ha", None, "wa"),
        P("ta", "ha", None, "wa"),
        P("ta", "ha", None, "wa"),
        P("wa", None),
        P(),
        P(("ta", "ha"), "wa"),
        P("wa", ("ta", "ha")),
        P("ta", "ha", None),
        P("ta", "ha", None, None),
    )
    return jax.shard_map(
        shards,
        mesh=mesh,
        in_specs=placed,
        out_specs=(
            P("ta", "ha", None, None),
            P("ta", "ha", None, "wa"),
            P("ta", "ha", None, "wa"),
            P("ta", "ha", None, "wa"),
            P("wa", ("ta", "ha")),
        ),
        check_vma=False,
    )
```

profile of v0, /device:TPU:0, one launch (start us, length us, event | category | flops | bytes accessed | tf_op | source)
XLA Modules:
  0.0 549.1 jit_solution(6073854629250690570)
XLA Ops:
  7.2 5.1 collective-permute-start.8
  13.6 4.6 collective-permute-start.4
  20.9 3.0 collective-permute-done.9
  23.9 4.4 collective-permute-start.10
  30.7 6.4 %collective-permute-start.6 = (bf16[3,1,384,384]{3,2,1,0:T(8,128)(2,1)S(1)}, bf16[3,1,384,384]{3,2,1,0:T(8,128)(2,1)}, u32[]{:S(2)}, u32[]{:S(2)}) collective-permute-start(bf16[3,1,384,384]{3,2,1,0:T(8,128)(2,1)S(1)} %constant_dynamic-update-slice_fusion.1), channel_id=1, source_target_pairs={{0,4},{1,5},{2,6},{3,7},{8,12},{9,13},{10,14},{11,15},{16,20},{17,... | collective-permute-start | bytes 2654216 | tf_op jit(solution)/shard_map/ppermute | solution.py:26
  39.0 4.8 collective-permute-start
  45.6 4.1 collective-permute-done.1
  51.0 5.5 collective-permute-start.2
  56.6 6.5 %collective-permute-done.2 = bf16[3,1,1]{0,2,1:T(2,128)(2,1)S(1)} collective-permute-done((bf16[3,1,1]{0,2,1:T(2,128)(2,1)S(1)}, bf16[3,1,1]{0,2,1:T(2,128)(2,1)S(1)}, u32[]{:S(2)}, u32[]{:S(2)}) %collective-permute-start.2) | collective-permute-done | bytes 38 | tf_op jit(solution)/shard_map/ppermute | solution.py:26
  64.5 4.0 collective-permute-done.3
  68.8 3.3 pad_maximum_fusion.1
  72.1 7.7 %reshape.147 = bf16[3456,3,128]{2,1,0:T(4,128)(2,1)} reshape(bf16[3,3,384,384]{3,2,1,0:T(8,128)(2,1)} %pad_maximum_fusion.1) | data formatting | bytes 5308416 | tf_op jit(solution)/shard_map/while/body/eval_jaxpr/reshape | solution.py:106
  79.8 3.9 copy.47
  83.7 3.3 pad_maximum_fusion
  87.0 7.7 %reshape.146 = bf16[3456,3,128]{2,1,0:T(4,128)(2,1)} reshape(bf16[3,3,384,384]{3,2,1,0:T(8,128)(2,1)} %pad_maximum_fusion) | data formatting | bytes 5308416 | tf_op jit(solution)/shard_map/while/body/eval_jaxpr/reshape | solution.py:105
  94.7 3.9 copy.46
  98.7 16.9 %while.44 = (s32[]{:T(128)}, f32[3,384,128]{1,2,0:T(8,128)S(1)}, bf16[3,384,128]{2,1,0:T(8,128)(2,1)S(1)}, bf16[3,3456,128]{2,1,0:T(8,128)(2,1)}, bf16[3,3456,128]{2,1,0:T(8,128)(2,1)}, /*index=5*/f32[9]{0:T(128)S(1)}, s32[]{:T(128)}) while((s32[]{:T(128)}, f32[3,384,128]{1,2,0:T(8,128)S(1)}, bf16[3,384,128]{2,1,0:T(8,128)(2,1)S(1)}, ...), condition=%wide.region_3.4_spmd.clone, body=%wide.region_0.3_spmd.clone.sunk | while | flops 690093312 | bytes 18014980 | solution.py:129
  101.8 2.5 fusion.112
  107.5 2.5 fusion.112
  113.1 2.5 fusion.112
  118.0 32.4 %reduce-scatter.4.cloned.1.call-done = f32[96,1536]{1,0:T(8,128)} async-done(((f32[384,1536]{1,0:T(8,128)}), f32[96,1536]{1,0:T(8,128)}) %reduce-scatter.4.cloned.1.call-update) | async-done | bytes 589840 | tf_op jit(solution)/shard_map/reduce_scatter | solution.py:136
  154.4 16.1 %all-gather.7.cloned.1.call-done = bf16[384,1536]{1,0:T(8,128)(2,1)} async-done(((bf16[96,1536]{1,0:T(8,128)(2,1)}), bf16[384,1536]{1,0:T(8,128)(2,1)}) %all-gather.7.cloned.1.call-update) | async-done | bytes 1179664 | tf_op jit(solution)/shard_map/all_gather | solution.py:147
  170.5 82.3 %all-gather.9.cloned.1.call-done = bf16[1536,1536]{1,0:T(8,128)(2,1)} async-done(((bf16[192,1536]{1,0:T(8,128)(2,1)}), bf16[1536,1536]{1,0:T(8,128)(2,1)}) %all-gather.9.cloned.1.call-update) | async-done | bytes 4718608 | tf_op jit(solution)/shard_map/all_gather | solution.py:149
  252.8 6.1 %fusion.80 = f32[384,1536]{1,0:T(8,128)} fusion(bf16[384,1536]{1,0:T(8,128)(2,1)} %all-gather.7.cloned.1.call-done, bf16[1536,1536]{1,0:T(8,128)(2,1)} %all-gather.9.cloned.1.call-done), kind=kOutput, calls=%fused_computation.124 | convolution fusion | flops 1811939328 | bytes 8257536 | tf_op jit(solution)/shard_map/dot_general | solution.py:152
  258.9 74.3 %all-gather.5.cloned.1.call-done = bf16[1536,1536]{0,1:T(8,128)(2,1)} async-done(((bf16[1536,192]{0,1:T(8,128)(2,1)}), bf16[1536,1536]{0,1:T(8,128)(2,1)}) %all-gather.5.cloned.1.call-update) | async-done | bytes 4718608 | tf_op jit(solution)/shard_map/all_gather | solution.py:150
  333.1 10.0 %fusion.56 = f32[384,1536]{1,0:T(8,128)} fusion(bf16[1536,1536]{1,0:T(8,128)(2,1)} %all-gather.9.cloned.1.call-done, bf16[1536,1536]{0,1:T(8,128)(2,1)} %all-gather.5.cloned.1.call-done, f32[384,1536]{1,0:T(8,128)} %fusion.80, bf16[1,1,384,1536]{3,2,1,0:T(8,128)(2,1)} %param.23), kind=kOutput, calls=%fused_computation.75 | convolution fusion | flops 3635085312 | bytes 15335424 | tf_op jit(solution)/shard_map/tf,df->td/dot_general | solution.py:155
  343.3 31.3 %reduce-scatter.6.cloned.1.call-done = f32[96,1536]{1,0:T(8,128)} async-done(((f32[384,1536]{1,0:T(8,128)}), f32[96,1536]{1,0:T(8,128)}) %reduce-scatter.6.cloned.1.call-update) | async-done | bytes 589840 | tf_op jit(solution)/shard_map/reduce_scatter | solution.py:156
  378.2 17.5 %all-gather.11.cloned.1.call-done = bf16[384,1536]{1,0:T(8,128)(2,1)} async-done(((bf16[96,1536]{1,0:T(8,128)(2,1)}), bf16[384,1536]{1,0:T(8,128)(2,1)}) %all-gather.11.cloned.1.call-update) | async-done | bytes 1179664 | tf_op jit(solution)/shard_map/all_gather | solution.py:161
  400.5 43.7 %while.45 = (s32[]{:T(128)}, bf16[3,384,128]{1,2,0:T(8,128)(2,1)S(1)}, bf16[3,3456,128]{2,1,0:T(8,128)(2,1)}, bf16[3,3456,128]{2,1,0:T(8,128)(2,1)}, bf16[3,384,...) while((s32[]{:T(128)}, ...), condition=%wide.region_14.15_spmd.clone, body=%wide.region_10.14_spmd.clone.sunk | while | flops 1723513728 | bytes 71701848 | solution.py:200
  405.9 2.5 multiply_reduce_fusion.5
  420.4 2.5 multiply_reduce_fusion.5
  435.1 2.5 multiply_reduce_fusion.5
  444.2 2.9 fusion.77
  447.1 5.5 copy.58
  456.1 5.6 %copy.59 = bf16[1152,3,128]{2,1,0:T(4,128)(2,1)S(1)} copy(bf16[1152,3,128]{2,0,1:T(8,128)(2,1)} %get-tuple-element.257) | data formatting | bytes 1769472 | tf_op jit(solution)/shard_map/slice | solution.py:229
  463.7 5.5 collective-permute-start.17
  469.1 3.4 fusion.78
  472.6 5.5 copy.55
  481.3 5.6 %copy.56 = bf16[1152,3,128]{2,1,0:T(4,128)(2,1)S(1)} copy(bf16[1152,3,128]{2,0,1:T(8,128)(2,1)} %get-tuple-element.260) | data formatting | bytes 1769472 | tf_op jit(solution)/shard_map/slice | solution.py:229
  488.9 5.7 %collective-permute-start.13 = (bf16[3,384,384]{2,1,0:T(8,128)(2,1)}, bf16[3,384,384]{2,1,0:T(8,128)(2,1)}, u32[]{:S(2)}, u32[]{:S(2)}) collective-permute-start(bf16[3,384,384]{2,1,0:T(8,128)(2,1)} %squeeze.56), channel_id=1, source_target_pairs={{0,8},{8,16},{16,24},{1,9},{9,17},{17,25},{2,10},{10,18},{18,26},{... | collective-permute-start | bytes 2654216 | tf_op jit(solution)/shard_map/ppermute | solution.py:38
  494.6 5.9 %copy.57 = f32[1152,3,128]{2,1,0:T(4,128)} copy(f32[1152,3,128]{2,0,1:T(8,128)S(1)} %get-tuple-element.258) | data formatting | bytes 3538944 | tf_op jit(solution)/shard_map/convert_element_type | solution.py:226
  500.5 4.3 reshape.158
  504.8 5.9 %copy.54 = f32[1152,3,128]{2,1,0:T(4,128)} copy(f32[1152,3,128]{2,0,1:T(8,128)S(1)} %copy-done.2) | data formatting | bytes 3538944 | tf_op jit(solution)/shard_map/convert_element_type | solution.py:225
  510.7 3.0 reshape.157
  513.7 3.5 fusion.72
  519.3 5.3 collective-permute-start.19
  524.6 2.9 fusion.73
  529.6 5.3 collective-permute-start.15
  (158 shorter events, 94.4 us)
Async XLA Ops:
  7.2 108.5 %copy-start = (bf16[384,1536]{1,0:T(8,128)(2,1)S(1)}, bf16[384,1536]{1,0:T(8,128)(2,1)}, u32[]{:S(2)}) copy-start(bf16[384,1536]{1,0:T(8,128)(2,1)} %param.18) | copy-start | bytes 3538948
  7.2 36.6 %copy-start.8 = (bf16[1,1,384,384]{3,2,1,0:T(8,128)(2,1)S(1)}, bf16[1,1,384,384]{3,2,1,0:T(8,128)(2,1)}, u32[]{:S(2)}) copy-start(bf16[1,1,384,384]{3,2,1,0:T(8,128)(2,1)} %param.15) | copy-start | bytes 884740
  7.2 143.2 %reduce-scatter.4.cloned.1.call-start = ((), (), s32[]{:S(2)}) async-start(), calls=%async_computation.4 | async-start | bytes 2949120 | tf_op jit(solution)/shard_map/reduce_scatter | solution.py:136
  7.2 12.6 %collective-permute-start.8 = (bf16[1,1,384,384]{3,2,1,0:T(8,128)(2,1)}, bf16[1,1,384,384]{3,2,1,0:T(8,128)(2,1)S(1)}, u32[]{:S(2)}, u32[]{:S(2)}) collective-permute-start(bf16[1,1,384,384]{3,2,1,0:T(8,128)(2,1)} %param.17), channel_id=1, source_target_pairs={{0,8},{8,16},{16,24},{1,9},{9,17},{17,25},{2,10},{10,18},{18,26},{... | collective-permute-start | bytes 884744 | tf_op jit(solution)/shard_map/ppermute | solution.py:26
  12.3 11.5 %collective-permute-start.9 = (bf16[1,1,384,384]{3,2,1,0:T(8,128)(2,1)}, bf16[1,1,384,384]{3,2,1,0:T(8,128)(2,1)S(1)}, u32[]{:S(2)}, u32[]{:S(2)}) collective-permute-start(bf16[1,1,384,384]{3,2,1,0:T(8,128)(2,1)} %param.17), channel_id=1, source_target_pairs={{8,0},{16,8},{24,16},{9,1},{17,9},{25,17},{10,2},{18,10},{26,18},{... | collective-permute-start | bytes 884744 | tf_op jit(solution)/shard_map/ppermute | solution.py:28
  13.6 15.9 %collective-permute-start.4 = (bf16[1,1,384,384]{3,2,1,0:T(8,128)(2,1)}, bf16[1,1,384,384]{3,2,1,0:T(8,128)(2,1)S(1)}, u32[]{:S(2)}, u32[]{:S(2)}) collective-permute-start(bf16[1,1,384,384]{3,2,1,0:T(8,128)(2,1)} %param.16), channel_id=1, source_target_pairs={{0,8},{8,16},{16,24},{1,9},{9,17},{17,25},{2,10},{10,18},{18,26},{... | collective-permute-start | bytes 884744 | tf_op jit(solution)/shard_map/ppermute | solution.py:26
  18.2 12.4 %collective-permute-start.5 = (bf16[1,1,384,384]{3,2,1,0:T(8,128)(2,1)}, bf16[1,1,384,384]{3,2,1,0:T(8,128)(2,1)S(1)}, u32[]{:S(2)}, u32[]{:S(2)}) collective-permute-start(bf16[1,1,384,384]{3,2,1,0:T(8,128)(2,1)} %param.16), channel_id=1, source_target_pairs={{8,0},{16,8},{24,16},{9,1},{17,9},{25,17},{10,2},{18,10},{26,18},{... | collective-permute-start | bytes 884744 | tf_op jit(solution)/shard_map/ppermute | solution.py:28
  23.9 44.9 %collective-permute-start.10 = (bf16[3,1,384,384]{3,2,1,0:T(8,128)(2,1)S(1)}, bf16[3,1,384,384]{3,2,1,0:T(8,128)(2,1)}, u32[]{:S(2)}, u32[]{:S(2)}) collective-permute-start(bf16[3,1,384,384]{3,2,1,0:T(8,128)(2,1)S(1)} %constant_dynamic-update-slice_fusion.4), channel_id=1, source_target_pairs={{0,4},{1,5},{2,6},{3,7},{8,12},{9,13},{10,14},{11,15},{16,20},{17,... | collective-permute-start | bytes 2654216 | tf_op jit(solution)/shard_map/ppermute | solution.py:26
  28.3 40.5 %collective-permute-start.11 = (bf16[3,1,384,384]{3,2,1,0:T(8,128)(2,1)S(1)}, bf16[3,1,384,384]{3,2,1,0:T(8,128)(2,1)}, u32[]{:S(2)}, u32[]{:S(2)}) collective-permute-start(bf16[3,1,384,384]{3,2,1,0:T(8,128)(2,1)S(1)} %constant_dynamic-update-slice_fusion.4), channel_id=1, source_target_pairs={{4,0},{5,1},{6,2},{7,3},{12,8},{13,9},{14,10},{15,11},{20,16},{21,... | collective-permute-start | bytes 2654216 | tf_op jit(solution)/shard_map/ppermute | solution.py:28
  30.7 53.0 %collective-permute-start.6 = (bf16[3,1,384,384]{3,2,1,0:T(8,128)(2,1)S(1)}, bf16[3,1,384,384]{3,2,1,0:T(8,128)(2,1)}, u32[]{:S(2)}, u32[]{:S(2)}) collective-permute-start(bf16[3,1,384,384]{3,2,1,0:T(8,128)(2,1)S(1)} %constant_dynamic-update-slice_fusion.1), channel_id=1, source_target_pairs={{0,4},{1,5},{2,6},{3,7},{8,12},{9,13},{10,14},{11,15},{16,20},{17,... | collective-permute-start | bytes 2654216 | tf_op jit(solution)/shard_map/ppermute | solution.py:26
  37.1 46.6 %collective-permute-start.7 = (bf16[3,1,384,384]{3,2,1,0:T(8,128)(2,1)S(1)}, bf16[3,1,384,384]{3,2,1,0:T(8,128)(2,1)}, u32[]{:S(2)}, u32[]{:S(2)}) collective-permute-start(bf16[3,1,384,384]{3,2,1,0:T(8,128)(2,1)S(1)} %constant_dynamic-update-slice_fusion.1), channel_id=1, source_target_pairs={{4,0},{5,1},{6,2},{7,3},{12,8},{13,9},{14,10},{15,11},{20,16},{21,... | collective-permute-start | bytes 2654216 | tf_op jit(solution)/shard_map/ppermute | solution.py:28
  39.0 5.2 collective-permute-start
  44.3 5.4 collective-permute-start.1
  51.0 12.1 %collective-permute-start.2 = (bf16[3,1,1]{0,2,1:T(2,128)(2,1)S(1)}, bf16[3,1,1]{0,2,1:T(2,128)(2,1)S(1)}, u32[]{:S(2)}, u32[]{:S(2)}) collective-permute-start(bf16[3,1,1]{0,2,1:T(2,128)(2,1)S(1)} %pad_maximum_fusion.2), channel_id=1, source_target_pairs={{0,4},{1,5},{2,6},{3,7},{8,12},{9,13},{10,14},{11,15},{16,20},{17,... | collective-permute-start | bytes 26 | tf_op jit(solution)/shard_map/ppermute | solution.py:26
  63.1 5.4 collective-permute-start.3
  94.7 3.9 copy-start.7
  117.9 34.0 %copy-start.9 = (f32[1536]{0:T(1024)S(1)}, f32[1536]{0:T(1024)}, u32[]{:S(2)}) copy-start(f32[1536]{0:T(1024)} %param.19) | copy-start | bytes 18436
  117.9 52.5 %all-gather.7.cloned.1.call-start = ((), (), s32[]{:S(2)}) async-start(), calls=%async_computation.5 | async-start | bytes 1474560 | tf_op jit(solution)/shard_map/all_gather | solution.py:147
  152.8 100.0 %all-gather.9.cloned.1.call-start = ((), (), s32[]{:S(2)}) async-start(), calls=%async_computation.6 | async-start | bytes 5308416 | tf_op jit(solution)/shard_map/all_gather | solution.py:149
  153.6 179.6 %all-gather.5.cloned.1.call-start = ((), (), s32[]{:S(2)}) async-start(), calls=%async_computation.3 | async-start | bytes 5308416 | tf_op jit(solution)/shard_map/all_gather | solution.py:150
  154.2 220.4 %reduce-scatter.6.cloned.1.call-start = ((), (), s32[]{:S(2)}) async-start(), calls=%async_computation.7 | async-start | bytes 2949120 | tf_op jit(solution)/shard_map/reduce_scatter | solution.py:156
  343.2 52.6 %all-gather.11.cloned.1.call-start = ((), (), s32[]{:S(2)}) async-start(), calls=%async_computation.8 | async-start | bytes 1474560 | tf_op jit(solution)/shard_map/all_gather | solution.py:161
  378.1 162.7 %reduce-scatter.8.cloned.1.call-start = ((), (), s32[]{:S(2)}) async-start(), calls=%async_computation.9 | async-start | bytes 2654208 | tf_op jit(solution)/shard_map/reduce_scatter | solution.py:165
  395.8 2.4 copy-start.3
  408.3 1.9 copy-start.5
  411.3 1.5 copy-start.6
  422.9 1.9 copy-start.5
  425.9 1.5 copy-start.6
  437.5 1.9 copy-start.5
  440.5 1.5 copy-start.6
  454.6 59.1 %collective-permute-start.16 = (bf16[3,384,384]{2,1,0:T(8,128)(2,1)}, bf16[3,384,384]{2,1,0:T(8,128)(2,1)}, u32[]{:S(2)}, u32[]{:S(2)}) collective-permute-start(bf16[3,384,384]{2,1,0:T(8,128)(2,1)} %squeeze.58), channel_id=1, source_target_pairs={{8,0},{16,8},{24,16},{9,1},{17,9},{25,17},{10,2},{18,10},{26,18},{... | collective-permute-start | bytes 2654216 | tf_op jit(solution)/shard_map/ppermute | solution.py:38
  463.7 50.0 %collective-permute-start.17 = (bf16[3,384,384]{2,1,0:T(8,128)(2,1)}, bf16[3,384,384]{2,1,0:T(8,128)(2,1)}, u32[]{:S(2)}, u32[]{:S(2)}) collective-permute-start(bf16[3,384,384]{2,1,0:T(8,128)(2,1)} %squeeze.59), channel_id=1, source_target_pairs={{0,8},{8,16},{16,24},{1,9},{9,17},{17,25},{2,10},{10,18},{18,26},{... | collective-permute-start | bytes 2654216 | tf_op jit(solution)/shard_map/ppermute | solution.py:38
  480.1 44.5 %collective-permute-start.12 = (bf16[3,384,384]{2,1,0:T(8,128)(2,1)}, bf16[3,384,384]{2,1,0:T(8,128)(2,1)}, u32[]{:S(2)}, u32[]{:S(2)}) collective-permute-start(bf16[3,384,384]{2,1,0:T(8,128)(2,1)} %squeeze.55), channel_id=1, source_target_pairs={{8,0},{16,8},{24,16},{9,1},{17,9},{25,17},{10,2},{18,10},{26,18},{... | collective-permute-start | bytes 2654216 | tf_op jit(solution)/shard_map/ppermute | solution.py:38
  488.9 35.7 %collective-permute-start.13 = (bf16[3,384,384]{2,1,0:T(8,128)(2,1)}, bf16[3,384,384]{2,1,0:T(8,128)(2,1)}, u32[]{:S(2)}, u32[]{:S(2)}) collective-permute-start(bf16[3,384,384]{2,1,0:T(8,128)(2,1)} %squeeze.56), channel_id=1, source_target_pairs={{0,8},{8,16},{16,24},{1,9},{9,17},{17,25},{2,10},{10,18},{18,26},{... | collective-permute-start | bytes 2654216 | tf_op jit(solution)/shard_map/ppermute | solution.py:38
  500.5 4.3 copy-start.2
  518.0 17.8 %collective-permute-start.18 = (bf16[384,384]{1,0:T(8,128)(2,1)}, bf16[384,384]{1,0:T(8,128)(2,1)S(1)}, u32[]{:S(2)}, u32[]{:S(2)}) collective-permute-start(bf16[384,384]{1,0:T(8,128)(2,1)} %get-tuple-element.262), channel_id=1, source_target_pairs={{4,0},{5,1},{6,2},{7,3},{12,8},{13,9},{14,10},{15,11},{20,16},{21,... | collective-permute-start | bytes 884744 | tf_op jit(solution)/shard_map/ppermute | solution.py:38
  519.3 16.5 %collective-permute-start.19 = (bf16[384,384]{1,0:T(8,128)(2,1)S(1)}, bf16[384,384]{1,0:T(8,128)(2,1)}, u32[]{:S(2)}, u32[]{:S(2)}) collective-permute-start(bf16[384,384]{1,0:T(8,128)(2,1)S(1)} %get-tuple-element.263), channel_id=1, source_target_pairs={{0,4},{1,5},{2,6},{3,7},{8,12},{9,13},{10,14},{11,15},{16,20},{17,... | collective-permute-start | bytes 884744 | tf_op jit(solution)/shard_map/ppermute | solution.py:38
  527.5 13.3 %copy-start.4 = (bf16[384,1536]{1,0:T(8,128)(2,1)S(1)}, bf16[384,1536]{1,0:T(8,128)(2,1)}, u32[]{:S(2)}) copy-start(bf16[384,1536]{1,0:T(8,128)(2,1)} %all-gather.11.cloned.1.call-done) | copy-start | bytes 3538948
  528.3 9.6 %collective-permute-start.14 = (bf16[384,384]{1,0:T(8,128)(2,1)}, bf16[384,384]{1,0:T(8,128)(2,1)S(1)}, u32[]{:S(2)}, u32[]{:S(2)}) collective-permute-start(bf16[384,384]{1,0:T(8,128)(2,1)} %get-tuple-element.264), channel_id=1, source_target_pairs={{4,0},{5,1},{6,2},{7,3},{12,8},{13,9},{14,10},{15,11},{20,16},{21,... | collective-permute-start | bytes 884744 | tf_op jit(solution)/shard_map/ppermute | solution.py:38
  529.6 9.3 %collective-permute-start.15 = (bf16[384,384]{1,0:T(8,128)(2,1)S(1)}, bf16[384,384]{1,0:T(8,128)(2,1)}, u32[]{:S(2)}, u32[]{:S(2)}) collective-permute-start(bf16[384,384]{1,0:T(8,128)(2,1)S(1)} %get-tuple-element.265), channel_id=1, source_target_pairs={{0,4},{1,5},{2,6},{3,7},{8,12},{9,13},{10,14},{11,15},{16,20},{17,... | collective-permute-start | bytes 884744 | tf_op jit(solution)/shard_map/ppermute | solution.py:38
  535.8 6.0 %copy-start.1 = (bf16[384,1536]{1,0:T(8,128)(2,1)S(1)}, bf16[384,1536]{1,0:T(8,128)(2,1)}, u32[]{:S(2)}) copy-start(bf16[384,1536]{1,0:T(8,128)(2,1)} %param.18) | copy-start | bytes 3538948
Sparse Core Ops, SparseCore 0:
  118.1 32.2 reduce-scatter.3
  153.0 17.4 all-gather.6
  172.9 79.8 all-gather.8
  255.1 78.0 all-gather.4
  343.3 31.1 reduce-scatter.5
  378.3 17.4 all-gather.10
  400.6 72.8 reduce-scatter.7
where the time goes:
time: 557 us; the launch traced here: 549 us
  waiting for transfers between devices  274 us (49%)
  local copies, waits for them, and re-layouts  84.7 us (15%)
  matrix products  66.8 us (12%)
  starting transfers between devices  65.9 us (12%)
  other arithmetic  41.6 us (7%)
  between operations  15.6 us (3%)
    all_gather x1, waiting for transfers between devices, shards(): lax.all_gather(up_weight, ('ta', 'ha'), axis=0, tiled=True)  82.3 us
    all_gather x1, waiting for transfers between devices, shards(): lax.all_gather(down_weight, ('ta', 'ha'), axis=1, tiled=True)  74.3 us
    reduce_scatter x1, waiting for transfers between devices, shards(): lax.psum_scatter(attn_part, 'wa', scatter_dimension=0, tiled=True)  32.4 us
    reduce_scatter x1, waiting for transfers between devices, shards(): lax.psum_scatter(norm_part, 'wa', scatter_dimension=0, tiled=True)  31.3 us
    ppermute x6, starting transfers between devices, extended(): lax.ppermute(tail, axis, [(i, (i + 1) % count) for i in range(ends)])  30.7 us
    ppermute x8, starting transfers between devices, from_behind(): return lax.ppermute(array, axis, pairs)  27.1 us
    all_gather x1, waiting for transfers between devices, shards(): stream_grad = lax.all_gather(grad_share, 'wa', axis=0, tiled=True)  17.5 us
    all_gather x1, waiting for transfers between devices, shards(): hidden_in = lax.all_gather(hidden_share, 'wa', axis=0, tiled=True)  16.1 us
  transfers between devices with their start and end apart: 27, of which 12 were waited for; matrix products, arithmetic and copies ran while one was open for 24% of the time, Pallas kernels for 0%

commit v1 on v0

--- a/solution.py
+++ b/solution.py
@@ -1,8 +1,11 @@
+import functools
 import math
 
 import jax
 import jax.numpy as jnp
 from jax import lax
+from jax.experimental import pallas as pl
+from jax.experimental.pallas import tpu as pltpu
 from jax.sharding import PartitionSpec as P
 
 HS = 128
@@ -253,6 +256,402 @@
     )
 
 
+MESH = pl.DeviceIdType.MESH
+WINDOW = 9
+CENTRE = 4
+
+
+def step_kernel(
+    n_t, n_h, n_w, kvm, q, stream, cot, ow, gain, upw, dnw,
+    sg, qg, kg, vg, wg,
+    kv, up, dn, score, top, total, probs, mix, att, apart, arecv, hid, normed, inv,
+    act, pgrad, npart, nrecv, gmask, wsend, wrecv, psend, precv,
+    halo_s, halo_r, wt_s, wt_r, r1_s, r1_r, a1_s, a1_r, r2_s, r2_r, a2_s, a2_r,
+    wg_s, wg_r, pt_s, pt_r,
+):
+    f32, bf16 = jnp.float32, jnp.bfloat16
+    t, h, w = lax.axis_index("ta"), lax.axis_index("ha"), lax.axis_index("wa")
+    n = n_t * n_h
+    g = t * n_h + h
+    rows, width = stream.shape
+    channels = q.shape[1]
+    heads = channels // HS
+    slab = upw.shape[0]
+    share = rows // n_w
+    hidden = upw.shape[1]
+    score_scale = 1.0 / math.sqrt(HS)
+    pending = []
+
+    def at_group(tt, hh):
+        return {"ta": tt, "ha": hh}
+
+    def at_wa(ww):
+        return {"wa": ww}
+
+    def group_peer(k):
+        idx = lax.rem(g + k, n)
+        return idx, at_group(idx // n_h, lax.rem(idx, n_h))
+
+    def send(src, dst, s_sem, r_sem, dev, cond=None):
+        copy = pltpu.make_async_remote_copy(
+            src_ref=src, dst_ref=dst, send_sem=s_sem, recv_sem=r_sem,
+            device_id=dev, device_id_type=MESH,
+        )
+        if cond is None:
+            copy.start()
+        else:
+            pl.when(cond)(copy.start)
+        pending.append((copy, cond))
+
+    def arrived(dst, s_sem, r_sem, dev, cond=None):
+        copy = pltpu.make_async_remote_copy(
+            src_ref=dst, dst_ref=dst, send_sem=s_sem, recv_sem=r_sem,
+            device_id=dev, device_id_type=MESH,
+        )
+        if cond is None:
+            copy.wait_recv()
+        else:
+            pl.when(cond)(copy.wait_recv)
+
+    def inside(tt, hh):
+        return (tt >= 0) & (tt < n_t) & (hh >= 0) & (hh < n_h)
+
+    def place(slot):
+        return t + slot // 3 - 1, h + slot % 3 - 1
+
+    def w_rows(ww):
+        return pl.ds(pl.multiple_of(ww * share, share), share)
+
+    def slab_rows(idx):
+        return pl.ds(pl.multiple_of(idx * slab, slab), slab)
+
+    barrier = pltpu.get_barrier_semaphore()
+    for k in range(1, n):
+        pl.semaphore_signal(barrier, inc=1, device_id=group_peer(k)[1], device_id_type=MESH)
+    for k in range(1, n_w):
+        pl.semaphore_signal(barrier, inc=1, device_id=at_wa(lax.rem(w + k, n_w)), device_id_type=MESH)
+    pl.semaphore_wait(barrier, n - 1 + n_w - 1)
+
+    for slot in (1, 7, 3, 5, 0, 2, 6, 8):
+        tt, hh = place(slot)
+        send(kvm, kv.at[8 - slot], halo_s.at[slot], halo_r.at[8 - slot], at_group(tt, hh), inside(tt, hh))
+
+    weights = (dn, up)
+
+    def hop(which, src_ref, idx, way):
+        tt, hh = ((t + 1, h), (t - 1, h), (t, h + 1), (t, h - 1))[way]
+        return (
+            src_ref, weights[which].at[slab_rows(idx)], wt_s.at[which, way, idx],
+            wt_r.at[which, idx], at_group(tt, hh),
+        ), inside(tt, hh)
+
+    def forward(which, src_ref, idx, ways, cond=None):
+        for way in ways:
+            args, here = hop(which, src_ref, idx, way)
+            send(*args, here if cond is None else here & cond)
+
+    forward(0, dnw, g, (2, 3, 0, 1))
+    forward(1, upw, g, (2, 3, 0, 1))
+
+    def relay(which, d):
+        for sign, way in ((1, 0), (-1, 1)):
+            tt = t - sign * d
+            cond = inside(tt, h)
+            idx = jnp.clip(tt, 0, n_t - 1) * n_h + h
+            block = weights[which].at[slab_rows(idx)]
+            arrived(block, wt_s.at[which, way, idx], wt_r.at[which, idx], at_group(t, h), cond)
+            forward(which, block, idx, (2, 3, way), cond)
+
+    def finish(which):
+        for e in range(1, n_h):
+            for sign, way in ((1, 2), (-1, 3)):
+                hh = h - sign * e
+                for d in range(-(n_t - 1), n_t):
+                    tt = t + d
+                    cond = inside(tt, hh)
+                    idx = jnp.clip(tt, 0, n_t - 1) * n_h + jnp.clip(hh, 0, n_h - 1)
+                    block = weights[which].at[slab_rows(idx)]
+                    arrived(block, wt_s.at[which, way, idx], wt_r.at[which, idx], at_group(t, h), cond)
+                    if e < n_h - 1:
+                        forward(which, block, idx, (way,), cond)
+
+    kv[CENTRE] = kvm[...]
+    dn[slab_rows(g), :] = dnw[...]
+    up[slab_rows(g), :] = upw[...]
+
+    for slot in (1, 7, 3, 5, 0, 2, 6, 8):
+        tt, hh = place(slot)
+        arrived(kv.at[slot], halo_s.at[slot], halo_r.at[slot], at_group(t, h), inside(tt, hh))
+
+    def each_tile(work):
+        @pl.loop(0, WINDOW)
+        def _(slot):
+            tt, hh = place(slot)
+            pl.when(inside(tt, hh))(lambda: work(slot))
+
+    nt = (((1,), (1,)), ((), ()))
+    tn = (((0,), (0,)), ((), ()))
+    key_rows, value_rows = pl.ds(0, TILE), pl.ds(TILE, TILE)
+    own_mark = kvm[pl.ds(2 * TILE, 1), :].astype(f32)
+
+    def attend(e):
+        cols = pl.ds(e * HS, HS)
+        top[...] = jnp.full(top.shape, NEG_FILL, f32)
+        total[...] = jnp.zeros(total.shape, f32)
+        mix[:, cols] = jnp.zeros((rows, HS), f32)
+
+        def raw(slot):
+            s = lax.dot_general(q[:, cols], kv[slot, key_rows, cols], nt, preferred_element_type=f32)
+            mark = kv[slot, pl.ds(2 * TILE, 1), :].astype(f32)
+            s = jnp.where(mark > 0.5, s * score_scale, NEG_FILL)
+            score[slot] = s
+            top[...] = jnp.maximum(top[...], jnp.max(s, axis=1, keepdims=True))
+
+        each_tile(raw)
+
+        def expo(slot):
+            p = jnp.exp(score[slot] - top[:, 0:1])
+            score[slot] = p
+            total[...] = total[...] + jnp.sum(p, axis=1, keepdims=True)
+
+        each_tile(expo)
+        total[...] = 1.0 / total[...]
+
+        def blend(slot):
+            p = (score[slot] * total[:, 0:1]).astype(bf16)
+            probs[e, slot] = p
+            mix[:, cols] = mix[:, cols] + jnp.dot(p, kv[slot, value_rows, cols], preferred_element_type=f32)
+
+        each_tile(blend)
+
+    for e in range(heads):
+        attend(e)
+        if e == heads - 2:
+            relay(0, 1)
+    att[...] = (mix[...] * own_mark).astype(bf16)
+    step = 512
+
+    def col_tiles(count, work):
+        @pl.loop(0, count // step)
+        def _(c):
+            work(pl.ds(pl.multiple_of(c * step, step), step))
+
+    def project(cols):
+        apart[:, cols] = jnp.dot(att[...], ow[:, cols], preferred_element_type=f32).astype(bf16)
+
+    col_tiles(width, project)
+    for k in range(1, n_w):
+        ww = lax.rem(w + k, n_w)
+        send(apart.at[w_rows(ww)], arecv.at[k], r1_s.at[k], r1_r.at[k], at_wa(ww))
+    relay(1, 1)
+    resid = stream[w_rows(w), :].astype(f32) + apart[w_rows(w), :].astype(f32)
+    for k in range(1, n_w):
+        arrived(arecv.at[k], r1_s.at[k], r1_r.at[k], at_wa(w))
+        resid = resid + arecv[k].astype(f32)
+    centered = resid - jnp.mean(resid, axis=1, keepdims=True)
+    istd = lax.rsqrt(jnp.mean(centered * centered, axis=1, keepdims=True) + EPSILON)
+    inv[...] = jnp.broadcast_to(istd, inv.shape)
+    normed[...] = centered * istd
+    hid[w_rows(w), :] = (normed[...] * gain[...]).astype(bf16)
+    for k in range(1, n_w):
+        send(hid.at[w_rows(w)], hid.at[w_rows(w)], a1_s.at[k], a1_r.at[k], at_wa(lax.rem(w + k, n_w)))
+    for d in range(2, n_t):
+        relay(0, d)
+        relay(1, d)
+    finish(0)
+
+    def act_tile(cols):
+        act[:, cols] = jnp.dot(cot[...], dn[:, cols], preferred_element_type=f32)
+
+    col_tiles(hidden, act_tile)
+    for k in range(1, n_w):
+        arrived(hid.at[w_rows(lax.rem(w + n_w - k, n_w))], a1_s.at[k], a1_r.at[k], at_wa(w))
+    finish(1)
+
+    def grad_tile(cols):
+        pre = jnp.dot(hid[...], up[:, cols], preferred_element_type=f32)
+        pgrad[:, cols] = (act[:, cols] * gelu_slope(pre)).astype(bf16)
+
+    col_tiles(hidden, grad_tile)
+    for c in range(width // step):
+        cols = pl.ds(c * step, step)
+        npart[:, cols] = lax.dot_general(
+            pgrad[...], up[cols, :], nt, preferred_element_type=f32
+        ).astype(bf16)
+        for k in range(1, n_w):
+            ww = lax.rem(w + k, n_w)
+            send(npart.at[w_rows(ww), cols], nrecv.at[k, :, cols], r2_s.at[c, k], r2_r.at[c, k], at_wa(ww))
+    for k in range(1, n_w):
+        for c in range(width // step):
+            arrived(nrecv.at[k, :, pl.ds(c * step, step)], r2_s.at[c, k], r2_r.at[c, k], at_wa(w))
+    ngrad = npart[w_rows(w), :].astype(f32)
+    for k in range(1, n_w):
+        ngrad = ngrad + nrecv[k].astype(f32)
+    back = norm_backward(ngrad, gain[...], normed[...], inv[:, 0:1])
+    sg[w_rows(w), :] = (cot[w_rows(w), :].astype(f32) + back).astype(bf16)
+    for k in range(1, n_w):
+        send(sg.at[w_rows(w)], sg.at[w_rows(w)], a2_s.at[k], a2_r.at[k], at_wa(lax.rem(w + k, n_w)))
+    for k in range(1, n_w):
+        arrived(sg.at[w_rows(lax.rem(w + n_w - k, n_w))], a2_s.at[k], a2_r.at[k], at_wa(w))
+
+    gmask[...] = (
+        lax.dot_general(sg[...], ow[...], nt, preferred_element_type=f32).astype(bf16).astype(f32)
+        * own_mark
+    ).astype(bf16)
+
+    def weight_tile(cols):
+        wsend[cols, :] = lax.dot_general(sg[:, cols], att[...], tn, preferred_element_type=f32).astype(bf16)
+
+    col_tiles(width, weight_tile)
+
+    def send_weight():
+        for k in range(1, n):
+            idx, dev = group_peer(k)
+            send(wsend.at[slab_rows(idx)], wrecv.at[k], wg_s.at[k], wg_r.at[k], dev)
+
+    def back_head(e):
+        cols = pl.ds(e * HS, HS)
+        grad = gmask[:, cols]
+        total[:, 0:1] = jnp.sum(grad.astype(f32) * mix[:, cols], axis=1, keepdims=True)
+        mix[:, cols] = jnp.zeros((rows, HS), f32)
+
+        def tile(slot):
+            p = probs[e, slot]
+            gp = lax.dot_general(gmask[:, cols], kv[slot, value_rows, cols], nt, preferred_element_type=f32)
+            ds = (p.astype(f32) * (gp - total[:, 0:1]) * score_scale).astype(bf16)
+            mix[:, cols] = mix[:, cols] + jnp.dot(ds, kv[slot, key_rows, cols], preferred_element_type=f32)
+            psend[slot, key_rows, cols] = lax.dot_general(
+                ds, q[:, cols], tn, preferred_element_type=f32
+            ).astype(bf16)
+            psend[slot, value_rows, cols] = lax.dot_general(
+                p, gmask[:, cols], tn, preferred_element_type=f32
+            ).astype(bf16)
+
+        each_tile(tile)
+        for slot in (0, 2, 6, 8, 1, 7, 3, 5):
+            tt, hh = place(slot)
+            send(
+                psend.at[slot, :, cols], precv.at[8 - slot, :, cols],
+                pt_s.at[e, slot], pt_r.at[e, 8 - slot], at_group(tt, hh), inside(tt, hh),
+            )
+
+    for e in range(heads):
+        back_head(e)
+        if e == 0:
+            send_weight()
+    qg[...] = mix[...].astype(bf16)
+    wsum = wsend[slab_rows(g), :].astype(f32)
+    for k in range(1, n):
+        arrived(wrecv.at[k], wg_s.at[k], wg_r.at[k], at_group(t, h))
+        wsum = wsum + wrecv[k].astype(f32)
+    wg[...] = wsum
+    for e in range(heads):
+        cols = pl.ds(e * HS, HS)
+        for slot in (0, 2, 6, 8, 1, 7, 3, 5):
+            tt, hh = place(slot)
+            arrived(precv.at[slot, :, cols], pt_s.at[e, slot], pt_r.at[e, slot], at_group(t, h), inside(tt, hh))
+    act[:, pl.ds(0, channels)] = psend[CENTRE, key_rows, :].astype(f32)
+    mix[...] = psend[CENTRE, value_rows, :].astype(f32)
+    for slot in (0, 1, 2, 3, 5, 6, 7, 8):
+        tt, hh = place(slot)
+
+        def gather(slot=slot):
+            act[:, pl.ds(0, channels)] = act[:, pl.ds(0, channels)] + precv[slot, key_rows, :].astype(f32)
+            mix[...] = mix[...] + precv[slot, value_rows, :].astype(f32)
+
+        pl.when(inside(tt, hh))(gather)
+    kg[...] = act[:, pl.ds(0, channels)].astype(bf16)
+    vg[...] = mix[...].astype(bf16)
+    for copy, cond in pending:
+        if cond is None:
+            copy.wait_send()
+        else:
+            pl.when(cond)(copy.wait_send)
+
+
+def fused_shards(
+    stream, queries, key_heads, value_heads, out_weight, norm_gain, up_weight, down_weight,
+    tile_route, cotangent,
+):
+    n_t, n_h, n_w = (lax.axis_size(a) for a in ("ta", "ha", "wa"))
+    n = n_t * n_h
+    rows, width = stream.shape[2:]
+    channels = queries.shape[3]
+    heads = channels // HS
+    slab, hidden = up_weight.shape
+    share = rows // n_w
+    bf16, f32 = jnp.bfloat16, jnp.float32
+    mark = jnp.broadcast_to(tile_route.reshape(1, 1).astype(bf16), (16, channels))
+    kvm = jnp.concatenate([key_heads.reshape(rows, channels), value_heads.reshape(rows, channels), mark], axis=0)
+    vm, dma = pltpu.VMEM, pltpu.SemaphoreType.DMA
+    tiles = width // 512
+    sg, qg, kg, vg, wg = pl.pallas_call(
+        functools.partial(step_kernel, n_t, n_h, n_w),
+        out_shape=[
+            jax.ShapeDtypeStruct((rows, width), bf16),
+            jax.ShapeDtypeStruct((rows, channels), bf16),
+            jax.ShapeDtypeStruct((rows, channels), bf16),
+            jax.ShapeDtypeStruct((rows, channels), bf16),
+            jax.ShapeDtypeStruct((slab, channels), f32),
+        ],
+        in_specs=[pl.BlockSpec(memory_space=vm)] * 8,
+        out_specs=[pl.BlockSpec(memory_space=vm)] * 5,
+        scratch_shapes=[
+            vm((WINDOW,) + kvm.shape, bf16),
+            vm((width, hidden), bf16),
+            vm((width, hidden), bf16),
+            vm((WINDOW, TILE, TILE), f32),
+            vm((rows, 128), f32),
+            vm((rows, 128), f32),
+            vm((heads, WINDOW, TILE, TILE), bf16),
+            vm((rows, channels), f32),
+            vm((rows, channels), bf16),
+            vm((rows, width), bf16),
+            vm((n_w, share, width), bf16),
+            vm((rows, width), bf16),
+            vm((share, width), f32),
+            vm((share, 128), f32),
+            vm((rows, hidden), f32),
+            vm((rows, hidden), bf16),
+            vm((rows, width), bf16),
+            vm((n_w, share, width), bf16),
+            vm((rows, channels), bf16),
+            vm((width, channels), bf16),
+            vm((n, slab, channels), bf16),
+            vm((WINDOW, 2 * TILE, channels), bf16),
+            vm((WINDOW, 2 * TILE, channels), bf16),
+            dma((WINDOW,)), dma((WINDOW,)),
+            dma((2, 4, n)), dma((2, n)),
+            dma((n_w,)), dma((n_w,)), dma((n_w,)), dma((n_w,)),
+            dma((tiles, n_w)), dma((tiles, n_w)), dma((n_w,)), dma((n_w,)),
+            dma((n,)), dma((n,)),
+            dma((heads, WINDOW)), dma((heads, WINDOW)),
+        ],
+        compiler_params=pltpu.CompilerParams(
+            collective_id=0, has_side_effects=True, vmem_limit_bytes=62 * 1024 * 1024
+        ),
+    )(
+        kvm, queries.reshape(rows, channels), stream.reshape(rows, width),
+        cotangent.reshape(rows, width), out_weight, norm_gain.reshape(1, width),
+        up_weight, down_weight.T,
+    )
+    cell = (1, 1, rows)
+    return (
+        sg.reshape(cell + (width,)),
+        qg.reshape(cell + (channels,)),
+        kg.reshape(cell + (channels,)),
+        vg.reshape(cell + (channels,)),
+        wg.T,
+    )
+
+
+def fits_kernel(mesh, stream, up_weight, tile_route):
+    n = mesh.shape["ta"] * mesh.shape["ha"]
+    slab = up_weight.shape[0] // n
+    share = stream.shape[2] // mesh.shape["wa"]
+    return slab % 16 == 0 and share % 16 == 0 and tile_route.shape[2] == 1 and stream.shape[3] % 512 == 0
+
+
 def solution(mesh):
     placed = (
         P("ta", "ha", None, None),
@@ -266,8 +665,12 @@
         P("ta", "ha", None),
         P("ta", "ha", None, None),
     )
-    return jax.shard_map(
-        shards,
+    def run(*args):
+        chosen = fused_shards if fits_kernel(mesh, args[0], args[6], args[8]) else shards
+        return placed_call(chosen)(*args)
+
+    placed_call = lambda body: jax.shard_map(
+        body,
         mesh=mesh,
         in_specs=placed,
         out_specs=(
@@ -279,3 +682,5 @@
         ),
         check_vma=False,
     )
+
+    return run

time: 557 us -> 245 us (0.44)
  the two profiles are of different devices: /device:TPU:0 before, /device:TPU:9 now
where the time goes in v1:
time: 245 us; the launch traced here: 244 us
  Pallas kernels  234 us (96%)
  local copies, waits for them, and re-layouts  6.6 us (3%)
    pallas_call x1, Pallas kernels, fused_shards(): pl.pallas_call(functools.partial(step_kernel, n_t, n_h, n_w), out_shape=[...  234 us
    unnamed x13, local copies, waits for them, and re-layouts  5.29 us

profile of v1, /device:TPU:9, one launch (start us, length us, event | category | flops | bytes accessed | tf_op | source)
XLA Modules:
  0.0 243.6 jit_solution(11879058602095614949)
XLA Ops:
  1.3 1.3 reshape.48.gain
  2.6 2.0 maximum_maximum_fusion.kvm
  4.6 233.6 %shard_map.137 = (bf16[384,1536]{1,0:T(8,128)(2,1)}, bf16[384,384]{1,0:T(8,128)(2,1)}, bf16[384,384]{1,0:T(8,128)(2,1)}, bf16[384,384]{1,0:T(8,128)(2,1)}, f32[192,384]{1,0:T(8,128)}) custom-call(bf16[784,384]{1,0:T(8,128)(2,1)} %maximum_maximum_fusion.kvm, bf16[384,384]{1,0:T(8,128)(2,1)} %bitcast.16, bf16[384,1536]{1,0:T(8,128)(2,1)} %bitcast.12, ...), custom_call_target="tpu_custom_call" | custom-call | tf_op jit(solution)/shard_map/pallas_call | solution.py:588
  238.3 0.0 copy-start.3
  238.3 0.0 copy-start.2
  238.3 2.4 copy.21
  240.7 0.0 copy-done.3
  240.7 0.0 copy-start.1
  240.7 0.0 copy-start
  240.7 0.7 copy.22
  241.4 0.0 copy-done.2
  241.4 0.7 copy.23
  242.1 0.0 copy-done.1
  242.2 0.7 copy.24
  242.9 0.0 copy-done
  242.9 0.7 copy.25
  (2 shorter events, 0.0 us)
Async XLA Ops:
  238.3 2.4 %copy-start.3 = (bf16[384,384]{1,0:T(8,128)(2,1)S(1)}, bf16[384,384]{1,0:T(8,128)(2,1)}, u32[]{:S(2)}) copy-start(bf16[384,384]{1,0:T(8,128)(2,1)} %get-tuple-element.11) | copy-start | bytes 884740
  238.3 3.2 %copy-start.2 = (bf16[384,384]{1,0:T(8,128)(2,1)S(1)}, bf16[384,384]{1,0:T(8,128)(2,1)}, u32[]{:S(2)}) copy-start(bf16[384,384]{1,0:T(8,128)(2,1)} %get-tuple-element.12) | copy-start | bytes 884740
  240.7 1.4 copy-start.1
  240.7 2.2 copy-start

commit v2 on v1

--- a/solution.py
+++ b/solution.py
@@ -325,6 +325,25 @@
     def slab_rows(idx):
         return pl.ds(pl.multiple_of(idx * slab, slab), slab)
 
+    pair = w + 1 - 2 * lax.rem(w, 2)
+    chips = n_w // 2
+
+    def gather_start(buf, s_sem, r_sem):
+        for k in range(1, chips):
+            ww = lax.rem(w + 2 * k, n_w)
+            send(buf.at[w_rows(w)], buf.at[w_rows(w)], s_sem.at[k], r_sem.at[k], at_wa(ww))
+        send(buf.at[w_rows(w)], buf.at[w_rows(w)], s_sem.at[0], r_sem.at[0], at_wa(pair))
+
+    def gather_end(buf, s_sem, r_sem):
+        for k in range(1, chips):
+            block = buf.at[w_rows(lax.rem(w + n_w - 2 * k, n_w))]
+            arrived(block, s_sem.at[k], r_sem.at[k], at_wa(w))
+            send(block, block, s_sem.at[chips + k], r_sem.at[chips + k], at_wa(pair))
+        arrived(buf.at[w_rows(pair)], s_sem.at[0], r_sem.at[0], at_wa(w))
+        for k in range(1, chips):
+            block = buf.at[w_rows(lax.rem(pair + n_w - 2 * k, n_w))]
+            arrived(block, s_sem.at[chips + k], r_sem.at[chips + k], at_wa(w))
+
     barrier = pltpu.get_barrier_semaphore()
     for k in range(1, n):
         pl.semaphore_signal(barrier, inc=1, device_id=group_peer(k)[1], device_id_type=MESH)
@@ -332,9 +351,17 @@
         pl.semaphore_signal(barrier, inc=1, device_id=at_wa(lax.rem(w + k, n_w)), device_id_type=MESH)
     pl.semaphore_wait(barrier, n - 1 + n_w - 1)
 
-    for slot in (1, 7, 3, 5, 0, 2, 6, 8):
+    def window_send(src, slot, tt, hh, cond):
+        send(src, kv.at[slot], halo_s.at[slot], halo_r.at[slot], at_group(tt, hh), cond)
+
+    def window_wait(slot):
         tt, hh = place(slot)
-        send(kvm, kv.at[8 - slot], halo_s.at[slot], halo_r.at[8 - slot], at_group(tt, hh), inside(tt, hh))
+        arrived(kv.at[slot], halo_s.at[slot], halo_r.at[slot], at_group(t, h), inside(tt, hh))
+
+    window_send(kvm, 3, t, h + 1, inside(t, h + 1))
+    window_send(kvm, 5, t, h - 1, inside(t, h - 1))
+    window_send(kvm, 1, t + 1, h, inside(t + 1, h))
+    window_send(kvm, 7, t - 1, h, inside(t - 1, h))
 
     weights = (dn, up)
 
@@ -350,8 +377,8 @@
             args, here = hop(which, src_ref, idx, way)
             send(*args, here if cond is None else here & cond)
 
-    forward(0, dnw, g, (2, 3, 0, 1))
-    forward(1, upw, g, (2, 3, 0, 1))
+    forward(0, dnw, g, (2, 3))
+    forward(1, upw, g, (2, 3))
 
     def relay(which, d):
         for sign, way in ((1, 0), (-1, 1)):
@@ -379,9 +406,15 @@
     dn[slab_rows(g), :] = dnw[...]
     up[slab_rows(g), :] = upw[...]
 
-    for slot in (1, 7, 3, 5, 0, 2, 6, 8):
-        tt, hh = place(slot)
-        arrived(kv.at[slot], halo_s.at[slot], halo_r.at[slot], at_group(t, h), inside(tt, hh))
+    for j in (0, 2):
+        window_wait(3 + j)
+        here = inside(t, h + j - 1)
+        window_send(kv.at[3 + j], j, t + 1, h, inside(t + 1, h) & here)
+        window_send(kv.at[3 + j], 6 + j, t - 1, h, inside(t - 1, h) & here)
+    forward(0, dnw, g, (0, 1))
+    forward(1, upw, g, (0, 1))
+    for slot in (1, 7, 0, 2, 6, 8):
+        window_wait(slot)
 
     def each_tile(work):
         @pl.loop(0, WINDOW)
@@ -453,8 +486,7 @@
     inv[...] = jnp.broadcast_to(istd, inv.shape)
     normed[...] = centered * istd
     hid[w_rows(w), :] = (normed[...] * gain[...]).astype(bf16)
-    for k in range(1, n_w):
-        send(hid.at[w_rows(w)], hid.at[w_rows(w)], a1_s.at[k], a1_r.at[k], at_wa(lax.rem(w + k, n_w)))
+    gather_start(hid, a1_s, a1_r)
     for d in range(2, n_t):
         relay(0, d)
         relay(1, d)
@@ -464,8 +496,7 @@
         act[:, cols] = jnp.dot(cot[...], dn[:, cols], preferred_element_type=f32)
 
     col_tiles(hidden, act_tile)
-    for k in range(1, n_w):
-        arrived(hid.at[w_rows(lax.rem(w + n_w - k, n_w))], a1_s.at[k], a1_r.at[k], at_wa(w))
+    gather_end(hid, a1_s, a1_r)
     finish(1)
 
     def grad_tile(cols):
@@ -473,26 +504,46 @@
         pgrad[:, cols] = (act[:, cols] * gelu_slope(pre)).astype(bf16)
 
     col_tiles(hidden, grad_tile)
+    def pair_sums(c):
+        cols = pl.ds(c * step, step)
+        for k in range(chips - 1, -1, -1):
+            block = nrecv.at[k, :, cols]
+            arrived(block, r2_s.at[c, k], r2_r.at[c, k], at_wa(w))
+            if k == 0:
+                continue
+            ww = lax.rem(w + 2 * k, n_w)
+            both = npart[w_rows(ww), cols].astype(f32) + nrecv[k, :, cols].astype(f32)
+            npart[w_rows(ww), cols] = both.astype(bf16)
+            send(
+                npart.at[w_rows(ww), cols], nrecv.at[chips + k, :, cols],
+                r2_s.at[c, chips + k], r2_r.at[c, chips + k], at_wa(ww),
+            )
+
     for c in range(width // step):
         cols = pl.ds(c * step, step)
         npart[:, cols] = lax.dot_general(
             pgrad[...], up[cols, :], nt, preferred_element_type=f32
         ).astype(bf16)
-        for k in range(1, n_w):
-            ww = lax.rem(w + k, n_w)
-            send(npart.at[w_rows(ww), cols], nrecv.at[k, :, cols], r2_s.at[c, k], r2_r.at[c, k], at_wa(ww))
-    for k in range(1, n_w):
+        for k in range(chips - 1, -1, -1):
+            ww = lax.rem(pair + 2 * k, n_w)
+            send(
+                npart.at[w_rows(ww), cols], nrecv.at[k, :, cols],
+                r2_s.at[c, k], r2_r.at[c, k], at_wa(pair),
+            )
+        if c >= 1:
+            pair_sums(c - 1)
+    pair_sums(width // step - 1)
+    for k in range(1, chips):
         for c in range(width // step):
-            arrived(nrecv.at[k, :, pl.ds(c * step, step)], r2_s.at[c, k], r2_r.at[c, k], at_wa(w))
-    ngrad = npart[w_rows(w), :].astype(f32)
-    for k in range(1, n_w):
-        ngrad = ngrad + nrecv[k].astype(f32)
+            at = chips + k
+            arrived(nrecv.at[at, :, pl.ds(c * step, step)], r2_s.at[c, at], r2_r.at[c, at], at_wa(w))
+    ngrad = npart[w_rows(w), :].astype(f32) + nrecv[0].astype(f32)
+    for k in range(1, chips):
+        ngrad = ngrad + nrecv[chips + k].astype(f32)
     back = norm_backward(ngrad, gain[...], normed[...], inv[:, 0:1])
     sg[w_rows(w), :] = (cot[w_rows(w), :].astype(f32) + back).astype(bf16)
-    for k in range(1, n_w):
-        send(sg.at[w_rows(w)], sg.at[w_rows(w)], a2_s.at[k], a2_r.at[k], at_wa(lax.rem(w + k, n_w)))
-    for k in range(1, n_w):
-        arrived(sg.at[w_rows(lax.rem(w + n_w - k, n_w))], a2_s.at[k], a2_r.at[k], at_wa(w))
+    gather_start(sg, a2_s, a2_r)
+    gather_end(sg, a2_s, a2_r)
 
     gmask[...] = (
         lax.dot_general(sg[...], ow[...], nt, preferred_element_type=f32).astype(bf16).astype(f32)
@@ -528,40 +579,80 @@
             ).astype(bf16)
 
         each_tile(tile)
-        for slot in (0, 2, 6, 8, 1, 7, 3, 5):
-            tt, hh = place(slot)
+        for j in (0, 2, 1):
+            for i in (0, 2):
+                tt, hh = t + i - 1, h + j - 1
+                land = (2 - i) * 3 + j
+                send(
+                    psend.at[i * 3 + j, :, cols], precv.at[land, :, cols],
+                    pt_s.at[e, land], pt_r.at[e, land], at_group(tt, h), inside(tt, hh),
+                )
+
+    def part_wait(e, slot):
+        tt, hh = place(slot)
+        block = precv.at[slot, :, pl.ds(e * HS, HS)]
+        arrived(block, pt_s.at[e, slot], pt_r.at[e, slot], at_group(t, h), inside(tt, hh))
+
+    def sum_time(e):
+        cols = pl.ds(e * HS, HS)
+        for j in (0, 2, 1):
+            here = inside(t, h + j - 1)
+            base = e * HS if j == 1 else 2 * channels
+            gap = channels if j == 1 else HS
+            key_acc, value_acc = pl.ds(base, HS), pl.ds(base + gap, HS)
+            for i in (0, 2):
+                part_wait(e, i * 3 + j)
+
+            def begin():
+                act[:, key_acc] = psend[3 + j, key_rows, cols].astype(f32)
+                act[:, value_acc] = psend[3 + j, value_rows, cols].astype(f32)
+
+            pl.when(here)(begin)
+            for i in (0, 2):
+
+                def add():
+                    act[:, key_acc] = act[:, key_acc] + precv[i * 3 + j, key_rows, cols].astype(f32)
+                    act[:, value_acc] = act[:, value_acc] + precv[i * 3 + j, value_rows, cols].astype(f32)
+
+                pl.when(inside(t + i - 1, h + j - 1))(add)
+            if j == 1:
+                continue
+
+            def settle():
+                psend[3 + j, key_rows, cols] = act[:, key_acc].astype(bf16)
+                psend[3 + j, value_rows, cols] = act[:, value_acc].astype(bf16)
+
+            pl.when(here)(settle)
             send(
-                psend.at[slot, :, cols], precv.at[8 - slot, :, cols],
-                pt_s.at[e, slot], pt_r.at[e, 8 - slot], at_group(tt, hh), inside(tt, hh),
+                psend.at[3 + j, :, cols], precv.at[5 - j, :, cols],
+                pt_s.at[e, 5 - j], pt_r.at[e, 5 - j], at_group(t, h + j - 1), here,
             )
 
+    send_weight()
     for e in range(heads):
         back_head(e)
-        if e == 0:
-            send_weight()
+        if e >= 1:
+            sum_time(e - 1)
     qg[...] = mix[...].astype(bf16)
+    sum_time(heads - 1)
     wsum = wsend[slab_rows(g), :].astype(f32)
     for k in range(1, n):
         arrived(wrecv.at[k], wg_s.at[k], wg_r.at[k], at_group(t, h))
         wsum = wsum + wrecv[k].astype(f32)
     wg[...] = wsum
-    for e in range(heads):
-        cols = pl.ds(e * HS, HS)
-        for slot in (0, 2, 6, 8, 1, 7, 3, 5):
-            tt, hh = place(slot)
-            arrived(precv.at[slot, :, cols], pt_s.at[e, slot], pt_r.at[e, slot], at_group(t, h), inside(tt, hh))
-    act[:, pl.ds(0, channels)] = psend[CENTRE, key_rows, :].astype(f32)
-    mix[...] = psend[CENTRE, value_rows, :].astype(f32)
-    for slot in (0, 1, 2, 3, 5, 6, 7, 8):
+    for slot in (3, 5):
+        for e in range(heads):
+            part_wait(e, slot)
         tt, hh = place(slot)
 
         def gather(slot=slot):
+            both = pl.ds(channels, channels)
             act[:, pl.ds(0, channels)] = act[:, pl.ds(0, channels)] + precv[slot, key_rows, :].astype(f32)
-            mix[...] = mix[...] + precv[slot, value_rows, :].astype(f32)
+            act[:, both] = act[:, both] + precv[slot, value_rows, :].astype(f32)
 
         pl.when(inside(tt, hh))(gather)
     kg[...] = act[:, pl.ds(0, channels)].astype(bf16)
-    vg[...] = mix[...].astype(bf16)
+    vg[...] = act[:, pl.ds(channels, channels)].astype(bf16)
     for copy, cond in pending:
         if cond is None:
             copy.wait_send()
@@ -649,7 +740,8 @@
     n = mesh.shape["ta"] * mesh.shape["ha"]
     slab = up_weight.shape[0] // n
     share = stream.shape[2] // mesh.shape["wa"]
-    return slab % 16 == 0 and share % 16 == 0 and tile_route.shape[2] == 1 and stream.shape[3] % 512 == 0
+    pairs = mesh.shape["wa"] % 2 == 0
+    return pairs and slab % 16 == 0 and share % 16 == 0 and tile_route.shape[2] == 1 and stream.shape[3] % 512 == 0
 
 
 def solution(mesh):

time: 245 us -> 217 us (0.89)
  Pallas kernels: 234 us -> 207 us
    pallas_call x1, Pallas kernels: 234 us -> 207 us  [fused_shards(): pl.pallas_call(functools.partial(step_kernel, n_t, n_h, n_w), out_shape=[...]
where the time goes in v2:
time: 217 us
  Pallas kernels  207 us (95%)
  local copies, waits for them, and re-layouts  6.6 us (3%)
    pallas_call x1, Pallas kernels, fused_shards(): pl.pallas_call(functools.partial(step_kernel, n_t, n_h, n_w), out_shape=[...  207 us
    unnamed x13, local copies, waits for them, and re-layouts  5.29 us

profile of v2, /device:TPU:9, one launch (start us, length us, event | category | flops | bytes accessed | tf_op | source)
XLA Modules:
  0.0 217.0 jit_solution(4108905700103316217)
XLA Ops:
  1.3 1.3 reshape.48.gain
  2.6 2.0 maximum_maximum_fusion.kvm
  4.6 207.1 %shard_map.137 = (bf16[384,1536]{1,0:T(8,128)(2,1)}, bf16[384,384]{1,0:T(8,128)(2,1)}, bf16[384,384]{1,0:T(8,128)(2,1)}, bf16[384,384]{1,0:T(8,128)(2,1)}, f32[192,384]{1,0:T(8,128)}) custom-call(bf16[784,384]{1,0:T(8,128)(2,1)} %maximum_maximum_fusion.kvm, bf16[384,384]{1,0:T(8,128)(2,1)} %bitcast.16, bf16[384,1536]{1,0:T(8,128)(2,1)} %bitcast.12, ...), custom_call_target="tpu_custom_call" | custom-call | tf_op jit(solution)/shard_map/pallas_call | solution.py:679
  211.7 0.0 copy-start.3
  211.7 0.0 copy-start.2
  211.8 2.4 %copy.21 = bf16[1,1,384,1536]{3,2,1,0:T(8,128)(2,1)} copy(bf16[1,1,384,1536]{3,2,1,0:T(8,128)(2,1)} %bitcast.14) | data formatting | bytes 2359296
  214.2 0.0 copy-done.3
  214.2 0.0 copy-start.1
  214.2 0.0 copy-start
  214.2 0.7 copy.22
  214.9 0.0 copy-done.2
  214.9 0.7 copy.23
  215.6 0.0 copy-done.1
  215.6 0.7 copy.24
  216.3 0.0 copy-done
  216.3 0.7 copy.25
  (2 shorter events, 0.0 us)
Async XLA Ops:
  211.7 2.4 %copy-start.3 = (bf16[384,384]{1,0:T(8,128)(2,1)S(1)}, bf16[384,384]{1,0:T(8,128)(2,1)}, u32[]{:S(2)}) copy-start(bf16[384,384]{1,0:T(8,128)(2,1)} %get-tuple-element.11) | copy-start | bytes 884740
  211.7 3.2 %copy-start.2 = (bf16[384,384]{1,0:T(8,128)(2,1)S(1)}, bf16[384,384]{1,0:T(8,128)(2,1)}, u32[]{:S(2)}) copy-start(bf16[384,384]{1,0:T(8,128)(2,1)} %get-tuple-element.12) | copy-start | bytes 884740
  214.2 1.4 copy-start.1
  214.2 2.2 copy-start

commit v3 on v2

--- a/solution.py
+++ b/solution.py
@@ -360,8 +360,6 @@
 
     window_send(kvm, 3, t, h + 1, inside(t, h + 1))
     window_send(kvm, 5, t, h - 1, inside(t, h - 1))
-    window_send(kvm, 1, t + 1, h, inside(t + 1, h))
-    window_send(kvm, 7, t - 1, h, inside(t - 1, h))
 
     weights = (dn, up)
 
@@ -377,7 +375,9 @@
             args, here = hop(which, src_ref, idx, way)
             send(*args, here if cond is None else here & cond)
 
-    forward(0, dnw, g, (2, 3))
+    forward(0, dnw, g, (0, 1, 2, 3))
+    window_send(kvm, 1, t + 1, h, inside(t + 1, h))
+    window_send(kvm, 7, t - 1, h, inside(t - 1, h))
     forward(1, upw, g, (2, 3))
 
     def relay(which, d):
@@ -411,8 +411,8 @@
         here = inside(t, h + j - 1)
         window_send(kv.at[3 + j], j, t + 1, h, inside(t + 1, h) & here)
         window_send(kv.at[3 + j], 6 + j, t - 1, h, inside(t - 1, h) & here)
-    forward(0, dnw, g, (0, 1))
     forward(1, upw, g, (0, 1))
+    relay(0, 1)
     for slot in (1, 7, 0, 2, 6, 8):
         window_wait(slot)
 
@@ -460,7 +460,7 @@
     for e in range(heads):
         attend(e)
         if e == heads - 2:
-            relay(0, 1)
+            relay(1, 1)
     att[...] = (mix[...] * own_mark).astype(bf16)
     step = 512
 
@@ -476,7 +476,8 @@
     for k in range(1, n_w):
         ww = lax.rem(w + k, n_w)
         send(apart.at[w_rows(ww)], arecv.at[k], r1_s.at[k], r1_r.at[k], at_wa(ww))
-    relay(1, 1)
+    if n_t > 2:
+        relay(0, 2)
     resid = stream[w_rows(w), :].astype(f32) + apart[w_rows(w), :].astype(f32)
     for k in range(1, n_w):
         arrived(arecv.at[k], r1_s.at[k], r1_r.at[k], at_wa(w))
@@ -488,7 +489,8 @@
     hid[w_rows(w), :] = (normed[...] * gain[...]).astype(bf16)
     gather_start(hid, a1_s, a1_r)
     for d in range(2, n_t):
-        relay(0, d)
+        if d > 2:
+            relay(0, d)
         relay(1, d)
     finish(0)
 
@@ -555,10 +557,36 @@
 
     col_tiles(width, weight_tile)
 
+    late = (n_h - 1) * n_t
+
+    def weight_slot(k, tt):
+        return (k - 1) * n_t + tt
+
     def send_weight():
-        for k in range(1, n):
-            idx, dev = group_peer(k)
-            send(wsend.at[slab_rows(idx)], wrecv.at[k], wg_s.at[k], wg_r.at[k], dev)
+        for tt in range(n_t):
+            for k in range(1, n_h):
+                hh = lax.rem(h + k, n_h)
+                at = weight_slot(k, tt)
+                send(
+                    wsend.at[slab_rows(tt * n_h + hh)], wrecv.at[at],
+                    wg_s.at[at], wg_r.at[at], at_group(t, hh),
+                )
+
+    def height_sum(tt):
+        both = wsend[slab_rows(tt * n_h + h), :].astype(f32)
+        for k in range(1, n_h):
+            both = both + wrecv[weight_slot(k, tt)].astype(f32)
+        return both
+
+    def relay_weight():
+        for at in range(late):
+            arrived(wrecv.at[at], wg_s.at[at], wg_r.at[at], at_group(t, h))
+        for k in range(1, n_t):
+            tt = lax.rem(t + k, n_t)
+            block = slab_rows(tt * n_h + h)
+            wsend[block, :] = height_sum(tt).astype(bf16)
+            at = late + k - 1
+            send(wsend.at[block], wrecv.at[at], wg_s.at[at], wg_r.at[at], at_group(tt, h))
 
     def back_head(e):
         cols = pl.ds(e * HS, HS)
@@ -631,14 +659,14 @@
     send_weight()
     for e in range(heads):
         back_head(e)
-        if e >= 1:
-            sum_time(e - 1)
+    relay_weight()
     qg[...] = mix[...].astype(bf16)
-    sum_time(heads - 1)
-    wsum = wsend[slab_rows(g), :].astype(f32)
-    for k in range(1, n):
-        arrived(wrecv.at[k], wg_s.at[k], wg_r.at[k], at_group(t, h))
-        wsum = wsum + wrecv[k].astype(f32)
+    for e in range(heads):
+        sum_time(e)
+    wsum = height_sum(t)
+    for at in range(late, late + n_t - 1):
+        arrived(wrecv.at[at], wg_s.at[at], wg_r.at[at], at_group(t, h))
+        wsum = wsum + wrecv[at].astype(f32)
     wg[...] = wsum
     for slot in (3, 5):
         for e in range(heads):

time: 217 us -> 204 us (0.940)
  Pallas kernels: 207 us -> 194 us
    pallas_call x1, Pallas kernels: 207 us -> 194 us  [fused_shards(): pl.pallas_call(functools.partial(step_kernel, n_t, n_h, n_w), out_shape=[...]
where the time goes in v3:
time: 204 us
  Pallas kernels  194 us (95%)
  local copies, waits for them, and re-layouts  6.6 us (3%)
  other arithmetic  2.04 us (1%)
    pallas_call x1, Pallas kernels, fused_shards(): pl.pallas_call(functools.partial(step_kernel, n_t, n_h, n_w), out_shape=[...  194 us
    unnamed x13, local copies, waits for them, and re-layouts  5.29 us

profile of v3, /device:TPU:9, one launch (start us, length us, event | category | flops | bytes accessed | tf_op | source)
XLA Modules:
  0.0 204.2 jit_solution(10881659989348331885)
XLA Ops:
  1.3 1.3 reshape.48.gain
  2.6 2.0 maximum_maximum_fusion.kvm
  4.6 194.3 %shard_map.137 = (bf16[384,1536]{1,0:T(8,128)(2,1)}, bf16[384,384]{1,0:T(8,128)(2,1)}, bf16[384,384]{1,0:T(8,128)(2,1)}, bf16[384,384]{1,0:T(8,128)(2,1)}, f32[192,384]{1,0:T(8,128)}) custom-call(bf16[784,384]{1,0:T(8,128)(2,1)} %maximum_maximum_fusion.kvm, bf16[384,384]{1,0:T(8,128)(2,1)} %bitcast.16, bf16[384,1536]{1,0:T(8,128)(2,1)} %bitcast.12, ...), custom_call_target="tpu_custom_call" | custom-call | tf_op jit(solution)/shard_map/pallas_call | solution.py:707
  198.9 0.0 copy-start.3
  198.9 0.0 copy-start.2
  198.9 2.4 %copy.21 = bf16[1,1,384,1536]{3,2,1,0:T(8,128)(2,1)} copy(bf16[1,1,384,1536]{3,2,1,0:T(8,128)(2,1)} %bitcast.14) | data formatting | bytes 2359296
  201.4 0.0 copy-done.3
  201.4 0.0 copy-start.1
  201.4 0.0 copy-start
  201.4 0.7 copy.22
  202.1 0.0 copy-done.2
  202.1 0.7 copy.23
  202.8 0.0 copy-done.1
  202.8 0.7 copy.24
  203.5 0.0 copy-done
  203.5 0.7 copy.25
  (2 shorter events, 0.0 us)
Async XLA Ops:
  198.9 2.4 %copy-start.3 = (bf16[384,384]{1,0:T(8,128)(2,1)S(1)}, bf16[384,384]{1,0:T(8,128)(2,1)}, u32[]{:S(2)}) copy-start(bf16[384,384]{1,0:T(8,128)(2,1)} %get-tuple-element.11) | copy-start | bytes 884740
  198.9 3.2 %copy-start.2 = (bf16[384,384]{1,0:T(8,128)(2,1)S(1)}, bf16[384,384]{1,0:T(8,128)(2,1)}, u32[]{:S(2)}) copy-start(bf16[384,384]{1,0:T(8,128)(2,1)} %get-tuple-element.12) | copy-start | bytes 884740
  201.4 1.4 copy-start.1
  201.4 2.2 %copy-start = (f32[192,384]{1,0:T(8,128)S(1)}, f32[192,384]{1,0:T(8,128)}, u32[]{:S(2)}) copy-start(f32[192,384]{1,0:T(8,128)} %get-tuple-element.14) | copy-start | bytes 884740

commit v4 on v3

--- a/solution.py
+++ b/solution.py
@@ -262,7 +262,7 @@
 
 
 def step_kernel(
-    n_t, n_h, n_w, kvm, q, stream, cot, ow, gain, upw, dnw,
+    n_t, n_h, n_w, keys, values, route, q, stream, cot, ow, gain, upw, dnw,
     sg, qg, kg, vg, wg,
     kv, up, dn, score, top, total, probs, mix, att, apart, arecv, hid, normed, inv,
     act, pgrad, npart, nrecv, gmask, wsend, wrecv, psend, precv,
@@ -344,6 +344,11 @@
             block = buf.at[w_rows(lax.rem(pair + n_w - 2 * k, n_w))]
             arrived(block, s_sem.at[chips + k], r_sem.at[chips + k], at_wa(w))
 
+    kvm = kv.at[CENTRE]
+    kv[CENTRE, pl.ds(0, TILE), :] = keys[...]
+    kv[CENTRE, pl.ds(TILE, TILE), :] = values[...]
+    own = jnp.full((16, channels), route[0, 0, 0], jnp.int32).astype(f32)
+    kv[CENTRE, pl.ds(2 * TILE, 16), :] = own.astype(bf16)
     barrier = pltpu.get_barrier_semaphore()
     for k in range(1, n):
         pl.semaphore_signal(barrier, inc=1, device_id=group_peer(k)[1], device_id_type=MESH)
@@ -402,7 +407,6 @@
                     if e < n_h - 1:
                         forward(which, block, idx, (way,), cond)
 
-    kv[CENTRE] = kvm[...]
     dn[slab_rows(g), :] = dnw[...]
     up[slab_rows(g), :] = upw[...]
 
@@ -425,7 +429,7 @@
     nt = (((1,), (1,)), ((), ()))
     tn = (((0,), (0,)), ((), ()))
     key_rows, value_rows = pl.ds(0, TILE), pl.ds(TILE, TILE)
-    own_mark = kvm[pl.ds(2 * TILE, 1), :].astype(f32)
+    own_mark = kv[CENTRE, pl.ds(2 * TILE, 1), :].astype(f32)
 
     def attend(e):
         cols = pl.ds(e * HS, HS)
@@ -486,7 +490,7 @@
     istd = lax.rsqrt(jnp.mean(centered * centered, axis=1, keepdims=True) + EPSILON)
     inv[...] = jnp.broadcast_to(istd, inv.shape)
     normed[...] = centered * istd
-    hid[w_rows(w), :] = (normed[...] * gain[...]).astype(bf16)
+    hid[w_rows(w), :] = (normed[...] * gain[...].reshape(1, width)).astype(bf16)
     gather_start(hid, a1_s, a1_r)
     for d in range(2, n_t):
         if d > 2:
@@ -542,7 +546,7 @@
     ngrad = npart[w_rows(w), :].astype(f32) + nrecv[0].astype(f32)
     for k in range(1, chips):
         ngrad = ngrad + nrecv[chips + k].astype(f32)
-    back = norm_backward(ngrad, gain[...], normed[...], inv[:, 0:1])
+    back = norm_backward(ngrad, gain[...].reshape(1, width), normed[...], inv[:, 0:1])
     sg[w_rows(w), :] = (cot[w_rows(w), :].astype(f32) + back).astype(bf16)
     gather_start(sg, a2_s, a2_r)
     gather_end(sg, a2_s, a2_r)
@@ -555,7 +559,6 @@
     def weight_tile(cols):
         wsend[cols, :] = lax.dot_general(sg[:, cols], att[...], tn, preferred_element_type=f32).astype(bf16)
 
-    col_tiles(width, weight_tile)
 
     late = (n_h - 1) * n_t
 
@@ -656,9 +659,11 @@
                 pt_s.at[e, 5 - j], pt_r.at[e, 5 - j], at_group(t, h + j - 1), here,
             )
 
-    send_weight()
     for e in range(heads):
         back_head(e)
+        if e == 0:
+            col_tiles(width, weight_tile)
+            send_weight()
     relay_weight()
     qg[...] = mix[...].astype(bf16)
     for e in range(heads):
@@ -700,8 +705,6 @@
     slab, hidden = up_weight.shape
     share = rows // n_w
     bf16, f32 = jnp.bfloat16, jnp.float32
-    mark = jnp.broadcast_to(tile_route.reshape(1, 1).astype(bf16), (16, channels))
-    kvm = jnp.concatenate([key_heads.reshape(rows, channels), value_heads.reshape(rows, channels), mark], axis=0)
     vm, dma = pltpu.VMEM, pltpu.SemaphoreType.DMA
     tiles = width // 512
     sg, qg, kg, vg, wg = pl.pallas_call(
@@ -713,10 +716,12 @@
             jax.ShapeDtypeStruct((rows, channels), bf16),
             jax.ShapeDtypeStruct((slab, channels), f32),
         ],
-        in_specs=[pl.BlockSpec(memory_space=vm)] * 8,
+        in_specs=[pl.BlockSpec(memory_space=vm)] * 2
+        + [pl.BlockSpec(memory_space=pltpu.SMEM)]
+        + [pl.BlockSpec(memory_space=vm)] * 7,
         out_specs=[pl.BlockSpec(memory_space=vm)] * 5,
         scratch_shapes=[
-            vm((WINDOW,) + kvm.shape, bf16),
+            vm((WINDOW, 2 * TILE + 16, channels), bf16),
             vm((width, hidden), bf16),
             vm((width, hidden), bf16),
             vm((WINDOW, TILE, TILE), f32),
@@ -750,8 +755,9 @@
             collective_id=0, has_side_effects=True, vmem_limit_bytes=62 * 1024 * 1024
         ),
     )(
-        kvm, queries.reshape(rows, channels), stream.reshape(rows, width),
-        cotangent.reshape(rows, width), out_weight, norm_gain.reshape(1, width),
+        key_heads.reshape(rows, channels), value_heads.reshape(rows, channels), tile_route,
+        queries.reshape(rows, channels), stream.reshape(rows, width),
+        cotangent.reshape(rows, width), out_weight, norm_gain,
         up_weight, down_weight.T,
     )
     cell = (1, 1, rows)

time: 204 us -> 200 us (0.980)
  other arithmetic: 2.04 us -> 0 us
    concatenate x1 -> x0, other arithmetic: 2.04 us -> none  [fused_shards(): jnp.concatenate([key_heads.reshape(rows, channels), value_heads.reshape(r...]
where the time goes in v4:
time: 200 us
  Pallas kernels  193 us (96%)
  local copies, waits for them, and re-layouts  5.29 us (3%)
    pallas_call x1, Pallas kernels, fused_shards(): pl.pallas_call(functools.partial(step_kernel, n_t, n_h, n_w), out_shape=[...  193 us
    unnamed x13, local copies, waits for them, and re-layouts  5.29 us

profile of v4, /device:TPU:9, one launch (start us, length us, event | category | flops | bytes accessed | tf_op | source)
XLA Modules:
  0.0 199.6 jit_solution(10368323036438225495)
XLA Ops:
  1.3 193.0 %shard_map.137 = (bf16[384,1536]{1,0:T(8,128)(2,1)}, bf16[384,384]{1,0:T(8,128)(2,1)}, bf16[384,384]{1,0:T(8,128)(2,1)}, bf16[384,384]{1,0:T(8,128)(2,1)}, f32[192,384]{1,0:T(8,128)}) custom-call(bf16[384,384]{1,0:T(8,128)(2,1)} %bitcast.15, bf16[384,384]{1,0:T(8,128)(2,1)} %bitcast.16, s32[1,1,1]{2,1,0:T(1,128)S(6)} %copy.20.route, ...), custom_call_target="tpu_custom_call" | custom-call | tf_op jit(solution)/shard_map/pallas_call | solution.py:710
  194.3 0.0 copy-start.3
  194.3 0.0 copy-start.2
  194.4 2.4 %copy.21 = bf16[1,1,384,1536]{3,2,1,0:T(8,128)(2,1)} copy(bf16[1,1,384,1536]{3,2,1,0:T(8,128)(2,1)} %bitcast.11) | data formatting | bytes 2359296
  196.8 0.0 copy-done.3
  196.8 0.0 copy-start.1
  196.8 0.0 copy-start
  196.8 0.7 copy.22
  197.5 0.0 copy-done.2
  197.5 0.7 copy.23
  198.2 0.0 copy-done.1
  198.2 0.7 copy.24
  198.9 0.0 copy-done
  198.9 0.7 copy.25
Async XLA Ops:
  194.3 2.4 %copy-start.3 = (bf16[384,384]{1,0:T(8,128)(2,1)S(1)}, bf16[384,384]{1,0:T(8,128)(2,1)}, u32[]{:S(2)}) copy-start(bf16[384,384]{1,0:T(8,128)(2,1)} %get-tuple-element.11) | copy-start | bytes 884740
  194.3 3.2 %copy-start.2 = (bf16[384,384]{1,0:T(8,128)(2,1)S(1)}, bf16[384,384]{1,0:T(8,128)(2,1)}, u32[]{:S(2)}) copy-start(bf16[384,384]{1,0:T(8,128)(2,1)} %get-tuple-element.12) | copy-start | bytes 884740
  196.8 1.4 copy-start.1
  196.8 2.2 %copy-start = (f32[192,384]{1,0:T(8,128)S(1)}, f32[192,384]{1,0:T(8,128)}, u32[]{:S(2)}) copy-start(f32[192,384]{1,0:T(8,128)} %get-tuple-element.14) | copy-start | bytes 884740

commit v5 on v4

--- a/solution.py
+++ b/solution.py
@@ -463,8 +463,10 @@
 
     for e in range(heads):
         attend(e)
-        if e == heads - 2:
+        if e == 0:
             relay(1, 1)
+    if n_t > 2:
+        relay(0, 2)
     att[...] = (mix[...] * own_mark).astype(bf16)
     step = 512
 
@@ -480,8 +482,6 @@
     for k in range(1, n_w):
         ww = lax.rem(w + k, n_w)
         send(apart.at[w_rows(ww)], arecv.at[k], r1_s.at[k], r1_r.at[k], at_wa(ww))
-    if n_t > 2:
-        relay(0, 2)
     resid = stream[w_rows(w), :].astype(f32) + apart[w_rows(w), :].astype(f32)
     for k in range(1, n_w):
         arrived(arecv.at[k], r1_s.at[k], r1_r.at[k], at_wa(w))

time: 200 us -> 200 us (level)
  no operation moved by 1% of the time
where the time goes in v5:
time: 200 us
  Pallas kernels  193 us (96%)
  local copies, waits for them, and re-layouts  5.29 us (3%)
    pallas_call x1, Pallas kernels, fused_shards(): pl.pallas_call(functools.partial(step_kernel, n_t, n_h, n_w), out_shape=[...  193 us
    unnamed x13, local copies, waits for them, and re-layouts  5.29 us

profile of v5, /device:TPU:9, one launch (start us, length us, event | category | flops | bytes accessed | tf_op | source)
XLA Modules:
  0.0 199.6 jit_solution(2487003992301740412)
XLA Ops:
  1.3 193.0 %shard_map.137 = (bf16[384,1536]{1,0:T(8,128)(2,1)}, bf16[384,384]{1,0:T(8,128)(2,1)}, bf16[384,384]{1,0:T(8,128)(2,1)}, bf16[384,384]{1,0:T(8,128)(2,1)}, f32[192,384]{1,0:T(8,128)}) custom-call(bf16[384,384]{1,0:T(8,128)(2,1)} %bitcast.15, bf16[384,384]{1,0:T(8,128)(2,1)} %bitcast.16, s32[1,1,1]{2,1,0:T(1,128)S(6)} %copy.20.route, ...), custom_call_target="tpu_custom_call" | custom-call | tf_op jit(solution)/shard_map/pallas_call | solution.py:710
  194.3 0.0 copy-start.3
  194.3 0.0 copy-start.2
  194.4 2.4 %copy.21 = bf16[1,1,384,1536]{3,2,1,0:T(8,128)(2,1)} copy(bf16[1,1,384,1536]{3,2,1,0:T(8,128)(2,1)} %bitcast.11) | data formatting | bytes 2359296
  196.8 0.0 copy-done.3
  196.8 0.0 copy-start.1
  196.8 0.0 copy-start
  196.8 0.7 copy.22
  197.5 0.0 copy-done.2
  197.5 0.7 copy.23
  198.2 0.0 copy-done.1
  198.2 0.7 copy.24
  198.9 0.0 copy-done
  198.9 0.7 copy.25
Async XLA Ops:
  194.3 2.4 %copy-start.3 = (bf16[384,384]{1,0:T(8,128)(2,1)S(1)}, bf16[384,384]{1,0:T(8,128)(2,1)}, u32[]{:S(2)}) copy-start(bf16[384,384]{1,0:T(8,128)(2,1)} %get-tuple-element.11) | copy-start | bytes 884740
  194.3 3.2 %copy-start.2 = (bf16[384,384]{1,0:T(8,128)(2,1)S(1)}, bf16[384,384]{1,0:T(8,128)(2,1)}, u32[]{:S(2)}) copy-start(bf16[384,384]{1,0:T(8,128)(2,1)} %get-tuple-element.12) | copy-start | bytes 884740
  196.8 1.4 copy-start.1
  196.8 2.2 %copy-start = (f32[192,384]{1,0:T(8,128)S(1)}, f32[192,384]{1,0:T(8,128)}, u32[]{:S(2)}) copy-start(f32[192,384]{1,0:T(8,128)} %get-tuple-element.14) | copy-start | bytes 884740
